TPU v7x, 256 devices: a whole 4x4x8 slice. The times are simulated.
256 devices in a mesh: gx: 8 (over x, core), gy: 32 (over z, y).
Axes of the slice: x: 4, y: 4, z: 8, core: 2. Of those that a mesh axis runs over, the one named last changes fastest.
Arguments:
- fields: bfloat16 [4, 2, 6144, 8192], P(None, None, 'gx', 'gy'), may hold values from -6 to 6
- parent: float32 [4, 2, 48, 48], replicated, may hold values from -6 to 6
- rate: float32 [4, 2], replicated, may hold values from 0.3 to 3
Outputs:
- tendency: bfloat16 [4, 2, 6144, 8192], P(None, None, 'gx', 'gy')
- spectra: float32 [4, 2, 48, 48], replicated
All inputs are finite; a program needn't handle non-finite values.
Results may differ from a plain program's by a relative error of at most 0.015.
Values may be sent and summed in bfloat16 or wider, within the bound.
No kernel may reach another device: no remote copies, remote signals or barrier semaphores. Data moves between devices by JAX's collectives and lax.ppermute only.
A program may use at most 64 MiB of HBM per device.

v0:
```python
import math

import jax
import jax.numpy as jnp
from jax import lax
from jax.sharding import PartitionSpec as P

KW = 24


def basis(start, count, total):
    positions = start + jnp.arange(count, dtype=jnp.int32)
    modes = jnp.arange(2 * KW, dtype=jnp.int32)
    wavenum = jnp.where(modes < KW, modes, modes - KW + 1)
    phase = (positions[:, None] * wavenum[None, :] % total).astype(jnp.float32) * (
        2.0 * math.pi / total
    )
    return jnp.where(modes[None, :] < KW, jnp.cos(phase), jnp.sin(phase))


def per_device(fields, parent, rate):
    count_x = lax.axis_size("gx")
    count_y = lax.axis_size("gy")
    fdim, ldim, cols_x, cols_y = fields.shape
    total_x = cols_x * count_x
    total_y = cols_y * count_y
    flat = fields.reshape(fdim * ldim, cols_x, cols_y)
    start_x = lax.axis_index("gx") * cols_x
    start_y = lax.axis_index("gy") * cols_y
    x_local = basis(start_x, cols_x, total_x)
    y_local = basis(start_y, cols_y, total_y)
    pencils = lax.all_to_all(flat, "gx", split_axis=2, concat_axis=1, tiled=True)
    narrow = pencils.shape[2]
    x_full = basis(0, total_x, total_x).astype(jnp.bfloat16)
    x_coeffs = jnp.einsum("fxy,xm->fmy", pencils, x_full, preferred_element_type=jnp.float32)
    y_rows = basis(start_y + lax.axis_index("gx") * narrow, narrow, total_y)
    partial_sum = jnp.einsum("fmy,yn->fmn", x_coeffs, y_rows, precision=lax.Precision.HIGHEST)
    totals = lax.psum(partial_sum, ("gx", "gy"))
    spectra = 2.0 / math.sqrt(total_x * total_y) * totals.reshape(fdim, ldim, 2 * KW, 2 * KW)
    delta = rate[:, :, None, None] * (parent - spectra)
    across = jnp.einsum(
        "fmn,yn->fmy",
        delta.reshape(fdim * ldim, 2 * KW, 2 * KW),
        y_local,
        precision=lax.Precision.HIGHEST,
    )
    whole = jnp.einsum("xm,fmy->fxy", x_local, across, precision=lax.Precision.HIGHEST)
    tendency = (whole / (2 * KW)).astype(jnp.bfloat16).reshape(fdim, ldim, cols_x, cols_y)
    return (tendency, spectra)


def solution(mesh):
    in_specs = (P(None, None, "gx", "gy"), P(), P())
    out_specs = (P(None, None, "gx", "gy"), P())
    return jax.shard_map(
        per_device, mesh=mesh, in_specs=in_specs, out_specs=out_specs, check_vma=False
    )
```

profile of v0, /device:TPU:1, one launch (start us, length us, event | category | flops | bytes accessed | tf_op | source)
XLA Modules:
  0.0 335.5 jit_solution(9950218353891847651)
XLA Ops:
  7.2 5.0 %copy.16 = bf16[8,768,256]{1,0,2:T(8,128)(2,1)} copy(bf16[8,768,256]{2,1,0:T(8,128)(2,1)} %bitcast.34) | data formatting | bytes 6291456 | tf_op jit(solution)/shard_map/reshape | solution.py:27
  12.1 6.8 %all-to-all-start = ((bf16[8,768,256]{1,0,2:T(8,128)(2,1)}), bf16[8,768,256]{1,0,2:T(8,128)(2,1)S(1)}, u32[]{:S(2)}, u32[]{:S(2)}) async-start(bf16[8,768,256]{1,0,2:T(8,128)(2,1)} %copy.16), calls=%async_computation | async-start | bytes 6291456 | tf_op jit(solution)/shard_map/all_to_all | solution.py:32
  18.9 0.0 all-reduce.2.cloned.1.call-start
  19.0 37.5 %all-to-all-done = bf16[8,768,256]{1,0,2:T(8,128)(2,1)S(1)} async-done(((bf16[8,768,256]{1,0,2:T(8,128)(2,1)}), bf16[8,768,256]{1,0,2:T(8,128)(2,1)S(1)}, u32[]{:S(2)}, u32[]{:S(2)}) %all-to-all-start) | async-done | bytes 3145760 | tf_op jit(solution)/shard_map/all_to_all | solution.py:32
  56.5 3.4 %copy.14 = bf16[8,8,768,32]{2,1,3,0:T(8,128)(2,1)} copy(bf16[8,8,768,32]{2,0,3,1:T(8,128)(2,1)S(1)} %bitcast.32) | data formatting | bytes 6291456 | tf_op jit(solution)/shard_map/all_to_all | solution.py:32
  59.9 4.2 %all_to_all.16 = bf16[8,6144,32]{1,2,0:T(8,128)(2,1)S(1)} reshape(bf16[8,8,768,32]{2,1,3,0:T(8,128)(2,1)} %copy.14) | data formatting | bytes 6291456 | tf_op jit(solution)/shard_map/all_to_all | solution.py:32
  64.1 0.0 copy-start.2
  64.1 0.0 copy-start.1
  64.1 5.5 %fusion.5 = f32[48,256]{0,1:S(1)} fusion(bf16[6144,256]{0,1:T(8,128)(2,1)S(1)} %bitcast.35, s32[48]{0:T(128)S(1)} %add_select_fusion.4, pred[48]{0:T(512)(128)(4,1)S(1)} %iota_compare_fusion), kind=kOutput, calls=%fused_computation.9 | convolution fusion | flops 154238976 | bytes 3195120
  69.6 1.3 fusion.50
  70.9 0.0 all-reduce.2.cloned.1.call-update
  70.9 0.0 copy-done.2
  70.9 0.1 copy.11
  71.0 246.4 %all-reduce.2.cloned.1.call-done = f32[8,48,48]{2,1,0:T(8,128)} async-done(((f32[8,48,48]{2,1,0:T(8,128)}), f32[8,48,48]{2,1,0:T(8,128)}) %all-reduce.2.cloned.1.call-update) | async-done | bytes 73744 | tf_op jit(solution)/shard_map/psum | solution.py:38
  317.5 0.9 broadcast_multiply_fusion
  318.4 0.0 copy-start
  318.4 0.0 copy-done.1
  318.4 0.1 subtract_multiply_fusion
  318.5 0.7 fusion.31
  319.2 6.6 %multiply_convert_fusion = bf16[8,256,768]{2,1,0:T(8,128)(2,1)S(1)} fusion(f32[8,48,256]{2,1,0:T(8,128)S(1)} %fusion.31, s32[48]{0:T(128)S(1)} %add_select_fusion.4, s32[768]{0:T(1024)S(1)} %iota_add_fusion, pred[48]{0:T(512)(128)(4,1)S(1)} %iota_compare_fusion), kind=kOutput, calls=%fused_computation | convolution fusion | flops 909484032 | bytes 3542256 | tf_op jit(solution)/shard_map/xm,fmy->fxy/dot_general | solution.py:47
  325.9 2.8 copy.15
  328.7 0.0 copy-done
  (5 shorter events, 0.0 us)
Async XLA Ops:
  12.1 44.4 %all-to-all-start = ((bf16[8,768,256]{1,0,2:T(8,128)(2,1)}), bf16[8,768,256]{1,0,2:T(8,128)(2,1)S(1)}, u32[]{:S(2)}, u32[]{:S(2)}) async-start(bf16[8,768,256]{1,0,2:T(8,128)(2,1)} %copy.16), calls=%async_computation | async-start | bytes 6291456 | tf_op jit(solution)/shard_map/all_to_all | solution.py:32
  18.9 298.5 %all-reduce.2.cloned.1.call-start = ((), (), s32[]{:S(2)}) async-start(), calls=%async_computation.1 | async-start | bytes 393216 | tf_op jit(solution)/shard_map/psum | solution.py:38
  64.1 6.8 %copy-start.2 = (f32[4,2]{0,1:T(2,128)S(1)}, f32[4,2]{0,1:T(2,128)}, u32[]{:S(2)}) copy-start(f32[4,2]{0,1:T(2,128)} %param.5) | copy-start | bytes 100
  64.1 254.3 %copy-start.1 = (f32[4,2,48,48]{3,2,1,0:T(8,128)S(1)}, f32[4,2,48,48]{3,2,1,0:T(8,128)}, u32[]{:S(2)}) copy-start(f32[4,2,48,48]{3,2,1,0:T(8,128)} %param.4) | copy-start | bytes 221188
  318.4 10.3 %copy-start = (f32[8,48,48]{2,1,0:T(8,128)}, f32[8,48,48]{2,1,0:T(8,128)S(1)}, u32[]{:S(2)}) copy-start(f32[8,48,48]{2,1,0:T(8,128)S(1)} %broadcast_multiply_fusion) | copy-start | bytes 221188
Sparse Core Ops, SparseCore 0:
  71.0 246.3 all-reduce.1
where the time goes:
time: 336 us
  waiting for transfers between devices  284 us (85%)
  local copies, waits for them, and re-layouts  15.4 us (5%)
  matrix products  14.1 us (4%)
  between operations  14.1 us (4%)
  starting transfers between devices  6.79 us (2%)
    psum x1, waiting for transfers between devices, per_device(): totals = lax.psum(partial_sum, ('gx', 'gy'))  246 us
    all_to_all x1, waiting for transfers between devices, per_device(): lax.all_to_all(flat, 'gx', split_axis=2, concat_axis=1, tiled=True)  37.5 us
    all_to_all x2, local copies, waits for them, and re-layouts, per_device(): lax.all_to_all(flat, 'gx', split_axis=2, concat_axis=1, tiled=True)  7.58 us
    all_to_all x1, starting transfers between devices, per_device(): lax.all_to_all(flat, 'gx', split_axis=2, concat_axis=1, tiled=True)  6.79 us
  transfers between devices with their start and end apart: 2, of which 2 were waited for; matrix products, arithmetic and copies ran while one was open for 0% of the time, Pallas kernels for 0%

commit v1 on v0

v1 whole, which is shorter than its diff:
```python
import math

import jax
import jax.numpy as jnp
import ml_dtypes
import numpy as np
from jax import lax
from jax.experimental import pallas as pl
from jax.experimental.pallas import tpu as pltpu
from jax.sharding import Mesh
from jax.sharding import PartitionSpec as P

KW = 24
MODES = 2 * KW
FLAT = 8
PIECE = 16
WIDTH = 3 * FLAT * PIECE
AXES = ("x", "c", "z", "y")
SIZES = {"x": 4, "c": 2, "z": 8, "y": 4}
CHIPS = [(x, y, z) for x in range(4) for y in range(4) for z in range(8)]


def basis(total):
    positions = np.arange(total, dtype=np.int64)
    modes = np.arange(MODES)
    wavenum = np.where(modes < KW, modes, modes - KW + 1)
    phase = (positions[:, None] * wavenum[None, :] % total) * (2.0 * math.pi / total)
    return np.where(modes[None, :] < KW, np.cos(phase), np.sin(phase)).astype(np.float32)


def halves(table):
    high = table.astype(ml_dtypes.bfloat16)
    low = (table - high.astype(np.float32)).astype(ml_dtypes.bfloat16)
    return high, low


def index_of(x, c, z, y):
    return ((x * 2 + c) * 8 + z) * 4 + y


def swap_cores():
    return [
        (index_of(x, c, z, y), index_of(x, 1 - c, z, y)) for x, y, z in CHIPS for c in (0, 1)
    ]


def hand_over(core, move):
    pairs = []
    for x, y, z in CHIPS:
        to_x, to_y, to_z = move(x, y, z)
        pairs.append((index_of(x, core, z, y), index_of(to_x, 1 - core, to_z, to_y)))
        pairs.append((index_of(x, 1 - core, z, y), index_of(x, core, z, y)))
    return pairs


def both(first, second):
    return lambda x, y, z: second(*first(x, y, z))


FLIP_X0 = lambda x, y, z: (x ^ 1, y, z)
FLIP_X1 = lambda x, y, z: (3 - x, y, z)
FLIP_Y0 = lambda x, y, z: (x, y ^ 1, z)
FLIP_Y1 = lambda x, y, z: (x, 3 - y, z)
FLIP_Z0 = lambda x, y, z: (x, y, z ^ 1)
FLIP_Z1 = lambda x, y, z: (x, y, z ^ 2)
FLIP_Z2 = lambda x, y, z: (x, y, 7 - z)
STAGES = ((FLIP_X0, FLIP_Y0), (FLIP_Z0, FLIP_Z1), (FLIP_X1, FLIP_Y1), (FLIP_Z2,))


def total_of(partial):
    core = 1
    half = partial.astype(jnp.bfloat16)
    running = half.astype(jnp.float32) + lax.ppermute(half, AXES, swap_cores()).astype(jnp.float32)
    for stage in STAGES:
        value = running.astype(jnp.bfloat16)
        moves = stage if len(stage) == 1 else (*stage, both(*stage))
        near = [lax.ppermute(value, AXES, hand_over(core, move)) for move in moves]
        own = lax.ppermute(value, AXES, swap_cores()).astype(jnp.float32)
        near = [part.astype(jnp.float32) for part in near]
        if len(near) == 1:
            running = own + near[0]
        else:
            running = (own + near[0]) + (near[1] + near[2])
        core = 1 - core
    other = lax.ppermute(running, AXES, swap_cores())
    return jnp.where(lax.axis_index("c") == core, running, other)


def mask_of(flat, rows):
    lane = lax.broadcasted_iota(jnp.int32, (rows, WIDTH), 1)
    return lane // PIECE % FLAT == flat


def dot(a, b, dims=((1,), (0,))):
    return lax.dot_general(a, b, (dims, ((), ())), preferred_element_type=jnp.float32)


def split(value):
    high = value.astype(jnp.bfloat16)
    return high, (value - high.astype(jnp.float32)).astype(jnp.bfloat16)


def where_am_i():
    gx = lax.axis_index("x") * 2 + lax.axis_index("c")
    gy = lax.axis_index("z") * 4 + lax.axis_index("y")
    return gx, gy


def analyse(scale, fields, x_tables, y_tables, out, blocks, x_table, y_table, high, low, sems):
    gx, gy = where_am_i()
    copy_y = pltpu.make_async_copy(y_tables.at[gy], y_table, sems.at[FLAT])
    copy_x = pltpu.make_async_copy(x_tables.at[gx], x_table, sems.at[FLAT + 1])
    copies = [
        pltpu.make_async_copy(fields.at[f // 2, f % 2], blocks.at[f], sems.at[f])
        for f in range(FLAT)
    ]
    copy_x.start()
    copies[0].start()
    copy_y.start()
    for copy in copies[1:]:
        copy.start()
    copy_x.wait()
    for f in range(FLAT):
        copies[f].wait()
        high[pl.ds(f * MODES, MODES)], low[pl.ds(f * MODES, MODES)] = split(
            dot(x_table[...], blocks[f])
        )
    copy_y.wait()
    row = lax.broadcasted_iota(jnp.int32, (WIDTH, MODES), 0)
    mode = lax.broadcasted_iota(jnp.int32, (WIDTH, MODES), 1)
    spread = (row // 128 * PIECE + row % PIECE == mode).astype(jnp.bfloat16)
    y_high = dot(spread, y_table[:MODES]).astype(jnp.bfloat16)
    y_low = dot(spread, y_table[MODES:]).astype(jnp.bfloat16)
    last = ((1,), (1,))
    product = (
        dot(high[...], y_high, last) + dot(low[...], y_high, last) + dot(high[...], y_low, last)
    )
    total = jnp.zeros((MODES, WIDTH), jnp.float32)
    for f in range(FLAT):
        total = jnp.where(mask_of(f, MODES), product[f * MODES : (f + 1) * MODES], total)
    out[...] = total * scale


def synthesise(sums, parent, rate, x_tables, y_tables, out, spectra, blocks, x_table, y_table, sems):
    gx, gy = where_am_i()
    copy_y = pltpu.make_async_copy(y_tables.at[gy], y_table, sems.at[FLAT])
    copy_x = pltpu.make_async_copy(x_tables.at[gx], x_table, sems.at[FLAT + 1])
    copy_y.start()
    copy_x.start()
    high, low = split(sums[...])
    none = jnp.zeros((MODES, WIDTH), jnp.bfloat16)
    highs = jnp.concatenate([jnp.where(mask_of(f, MODES), high, none) for f in range(FLAT)])
    lows = jnp.concatenate([jnp.where(mask_of(f, MODES), low, none) for f in range(FLAT)])
    row = lax.broadcasted_iota(jnp.int32, (WIDTH, MODES), 0)
    mode = lax.broadcasted_iota(jnp.int32, (WIDTH, MODES), 1)
    gather = (row // 128 * PIECE + row % PIECE == mode).astype(jnp.bfloat16)
    coeffs = dot(highs, gather) + dot(lows, gather)
    copy_y.wait()
    y_high, y_low = y_table[:MODES], y_table[MODES:]
    rows = []
    for f in range(FLAT):
        mine = coeffs[f * MODES : (f + 1) * MODES]
        spectra[f // 2, f % 2] = mine
        rows.append((rate[f // 2, f % 2] / MODES) * (parent[f // 2, f % 2] - mine))
    d_high, d_low = split(jnp.concatenate(rows))
    across = dot(d_high, y_high) + dot(d_low, y_high) + dot(d_high, y_low)
    a_high, a_low = split(across)
    copy_x.wait()
    copies = []
    for f in range(FLAT):
        mine = slice(f * MODES, (f + 1) * MODES)
        weights = jnp.concatenate([a_high[mine], a_high[mine], a_low[mine]])
        blocks[f] = dot(x_table[...], weights).astype(jnp.bfloat16)
        copy = pltpu.make_async_copy(blocks.at[f], out.at[f // 2, f % 2], sems.at[f])
        copy.start()
        copies.append(copy)
    for copy in copies:
        copy.wait()


def solution(mesh):
    fine = Mesh(mesh.devices.reshape(tuple(SIZES[a] for a in AXES)), AXES)
    total_x, total_y = 6144, 8192
    cols_x, cols_y = total_x // 8, total_y // 32
    x_high, x_low = halves(basis(total_x))
    y_high, y_low = halves(basis(total_y))
    narrow = x_high.reshape(8, cols_x, MODES).transpose(0, 2, 1)
    x_tables = np.concatenate([x_high, x_low, x_high], 1).reshape(8, cols_x, 3 * MODES)
    y_tables = np.concatenate(
        [t.reshape(32, cols_y, MODES).transpose(0, 2, 1) for t in (y_high, y_low)], 1
    )
    scale = 2.0 / math.sqrt(total_x * total_y)
    any_space = pl.BlockSpec(memory_space=pl.ANY)
    vmem = pl.BlockSpec(memory_space=pltpu.VMEM)
    grant = pltpu.CompilerParams(vmem_limit_bytes=24 * 1024 * 1024)

    def per_device(fields, parent, rate):
        partial = pl.pallas_call(
            lambda *refs: analyse(scale, *refs),
            out_shape=jax.ShapeDtypeStruct((MODES, WIDTH), jnp.float32),
            in_specs=[any_space] * 3,
            out_specs=vmem,
            scratch_shapes=[
                pltpu.VMEM((FLAT, cols_x, cols_y), jnp.bfloat16),
                pltpu.VMEM((MODES, cols_x), jnp.bfloat16),
                pltpu.VMEM((2 * MODES, cols_y), jnp.bfloat16),
                pltpu.VMEM((FLAT * MODES, cols_y), jnp.bfloat16),
                pltpu.VMEM((FLAT * MODES, cols_y), jnp.bfloat16),
                pltpu.SemaphoreType.DMA((FLAT + 2,)),
            ],
            compiler_params=grant,
            name="analyse",
        )(fields, jnp.asarray(narrow), jnp.asarray(y_tables))
        with jax.named_scope("total"):
            sums = total_of(partial)
        tendency, spectra = pl.pallas_call(
            synthesise,
            out_shape=(
                jax.ShapeDtypeStruct((4, 2, cols_x, cols_y), jnp.bfloat16),
                jax.ShapeDtypeStruct((4, 2, MODES, MODES), jnp.float32),
            ),
            in_specs=[vmem, vmem, pl.BlockSpec(memory_space=pltpu.SMEM), any_space, any_space],
            out_specs=(any_space, vmem),
            scratch_shapes=[
                pltpu.VMEM((FLAT, cols_x, cols_y), jnp.bfloat16),
                pltpu.VMEM((cols_x, 3 * MODES), jnp.bfloat16),
                pltpu.VMEM((2 * MODES, cols_y), jnp.bfloat16),
                pltpu.SemaphoreType.DMA((FLAT + 2,)),
            ],
            compiler_params=grant,
            name="synthesise",
        )(sums, parent, rate, jnp.asarray(x_tables), jnp.asarray(y_tables))
        return tendency, spectra

    grid = P(None, None, ("x", "c"), ("z", "y"))
    return jax.shard_map(
        per_device, mesh=fine, in_specs=(grid, P(), P()), out_specs=(grid, P()), check_vma=False
    )
```

time: 336 us -> 45.5 us (0.14)
  waiting for transfers between devices: 284 us -> 11.4 us
  matrix products: 14.1 us -> 0 us
  between operations: 14.1 us -> 0.73 us
  starting transfers between devices: 6.79 us -> 18.1 us
  local copies, waits for them, and re-layouts: 15.4 us -> 6.35 us
  Pallas kernels: 0 us -> 8.62 us
    psum x1 -> x0, waiting for transfers between devices: 246 us -> none  [per_device(): totals = lax.psum(partial_sum, ('gx', 'gy'))]
    all_to_all x1 -> x0, waiting for transfers between devices: 37.5 us -> none  [per_device(): lax.all_to_all(flat, 'gx', split_axis=2, concat_axis=1, tiled=True)]
    ppermute x0 -> x16, starting transfers between devices: none -> 18.1 us  [the longest x10 13.5 us: total_of(): near = [lax.ppermute(value, AXES, hand_over(core, move)) for move in moves]]
    ppermute x0 -> x16, waiting for transfers between devices: none -> 11.4 us  [the longest x10 9.05 us: total_of(): near = [lax.ppermute(value, AXES, hand_over(core, move)) for move in moves]]
    dot_general x3 -> x0, matrix products: 8.63 us -> none  [the longest x1 6.64 us: per_device(): jnp.einsum('xm,fmy->fxy', x_local, across, precision=lax.Precision.HIGHEST)]
    pallas_call x0 -> x2, Pallas kernels: none -> 8.62 us  [the longest x1 4.39 us: per_device(): pl.pallas_call(synthesise, out_shape=(jax.ShapeDtypeStruct((4, 2, cols_x,...]
    all_to_all x2 -> x0, local copies, waits for them, and re-layouts: 7.58 us -> none  [per_device(): lax.all_to_all(flat, 'gx', split_axis=2, concat_axis=1, tiled=True)]
    all_to_all x1 -> x0, starting transfers between devices: 6.79 us -> none  [per_device(): lax.all_to_all(flat, 'gx', split_axis=2, concat_axis=1, tiled=True)]
  transfers between devices with their start and end apart: 2 -> 16, of which waited for: 2 -> 13; matrix products, arithmetic and copies ran while one was open for 0% -> 0% of each run, Pallas kernels for 0% -> 0%
where the time goes in v1:
time: 45.5 us; the launch traced here: 45.2 us
  starting transfers between devices  18.1 us (40%)
  waiting for transfers between devices  11.4 us (25%)
  Pallas kernels  8.62 us (19%)
  local copies, waits for them, and re-layouts  6.35 us (14%)
  between operations  0.73 us (2%)
    ppermute x10, starting transfers between devices, total_of(): near = [lax.ppermute(value, AXES, hand_over(core, move)) for move in moves]  13.5 us
    ppermute x10, waiting for transfers between devices, total_of(): near = [lax.ppermute(value, AXES, hand_over(core, move)) for move in moves]  9.05 us
    unnamed x15, local copies, waits for them, and re-layouts  6.35 us
    pallas_call x1, Pallas kernels, per_device(): pl.pallas_call(synthesise, out_shape=(jax.ShapeDtypeStruct((4, 2, cols_x,...  4.39 us
    pallas_call x1, Pallas kernels, per_device(): pl.pallas_call(lambda *refs: analyse(scale, *refs), out_shape=jax.ShapeDt...  4.23 us
    ppermute x1, starting transfers between devices, total_of(): lax.ppermute(half, AXES, swap_cores()).astype(jnp.float32)  3.33 us
    ppermute x4, starting transfers between devices, total_of(): own = lax.ppermute(value, AXES, swap_cores()).astype(jnp.float32)  1.2 us
    ppermute x1, waiting for transfers between devices, total_of(): other = lax.ppermute(running, AXES, swap_cores())  1.14 us
  transfers between devices with their start and end apart: 16, of which 13 were waited for; matrix products, arithmetic and copies ran while one was open for 0% of the time, Pallas kernels for 0%

profile of v1, /device:TPU:1, one launch (start us, length us, event | category | flops | bytes accessed | tf_op | source)
XLA Modules:
  0.0 45.2 jit_solution(2504231313289382059)
XLA Ops:
  0.6 0.0 copy-start
  0.6 1.4 %copy-done = bf16[32,96,256]{2,1,0:T(8,128)(2,1)S(1)} copy-done((bf16[32,96,256]{2,1,0:T(8,128)(2,1)S(1)}, bf16[32,96,256]{2,1,0:T(8,128)(2,1)}, u32[]{:S(2)}) %copy-start) | copy-done | bytes 1572888
  2.0 0.0 copy-start.3
  2.0 1.9 %copy-done.3 = bf16[4,2,768,256]{3,2,1,0:T(8,128)(2,1)S(1)} copy-done((bf16[4,2,768,256]{3,2,1,0:T(8,128)(2,1)S(1)}, bf16[4,2,768,256]{3,2,1,0:T(8,128)(2,1)}, u32[]{:S(2)}) %copy-start.3) | copy-done | bytes 3145752
  3.9 0.0 copy-start.4
  3.9 1.1 %copy-done.4 = bf16[8,48,768]{2,1,0:T(8,128)(2,1)S(1)} copy-done((bf16[8,48,768]{2,1,0:T(8,128)(2,1)S(1)}, bf16[8,48,768]{2,1,0:T(8,128)(2,1)}, u32[]{:S(2)}) %copy-start.4) | copy-done | bytes 589848
  5.0 0.0 copy-start.6
  5.0 0.0 copy-start.1
  5.0 4.2 %analyse.1 = f32[48,384]{1,0:T(8,128)S(1)} custom-call(bf16[4,2,768,256]{3,2,1,0:T(8,128)(2,1)S(1)} %copy-done.3, bf16[8,48,768]{2,1,0:T(8,128)(2,1)S(1)} %copy-done.4, bf16[32,96,256]{2,1,0:T(8,128)(2,1)S(1)} %copy-done), custom_call_target="tpu_custom_call" | custom-call | tf_op jit(solution)/shard_map/analyse/pallas_call | solution.py:198
  9.3 3.3 %collective-permute-start = (bf16[48,384]{1,0:T(8,128)(2,1)S(1)}, bf16[48,384]{1,0:T(8,128)(2,1)S(1)}, u32[]{:S(2)}, u32[]{:S(2)}) collective-permute-start(bf16[48,384]{1,0:T(8,128)(2,1)S(1)} %convert_element_type.63), channel_id=1, source_target_pairs={{0,32},{32,0},{4,36},{36,4},{8,40},{40,8},{12,44},{44,12},{16,48},... | collective-permute-start | bytes 110600 | tf_op jit(solution)/shard_map/total/ppermute | solution.py:73
  12.6 0.9 %collective-permute-done = bf16[48,384]{1,0:T(8,128)(2,1)S(1)} collective-permute-done((bf16[48,384]{1,0:T(8,128)(2,1)S(1)}, bf16[48,384]{1,0:T(8,128)(2,1)S(1)}, u32[]{:S(2)}, u32[]{:S(2)}) %collective-permute-start) | collective-permute-done | bytes 36896 | tf_op jit(solution)/shard_map/total/ppermute | solution.py:73
  13.5 0.8 %collective-permute-start.4 = (bf16[48,384]{1,0:T(8,128)(2,1)S(1)}, bf16[48,384]{1,0:T(8,128)(2,1)S(1)}, u32[]{:S(2)}, u32[]{:S(2)}) collective-permute-start(bf16[48,384]{1,0:T(8,128)(2,1)S(1)} %add_convert_fusion.3), channel_id=1, source_target_pairs={{32,65},{0,32},{36,69},{4,36},{40,73},{8,40},{44,77},{12,44},{48,8... | collective-permute-start | bytes 110600 | tf_op jit(solution)/shard_map/total/ppermute | solution.py:77
  14.3 0.0 collective-permute-start.3
  14.3 0.6 %collective-permute-start.2 = (bf16[48,384]{1,0:T(8,128)(2,1)S(1)}, bf16[48,384]{1,0:T(8,128)(2,1)S(1)}, u32[]{:S(2)}, u32[]{:S(2)}) collective-permute-start(bf16[48,384]{1,0:T(8,128)(2,1)S(1)} %add_convert_fusion.3), channel_id=1, source_target_pairs={{32,64},{0,32},{36,68},{4,36},{40,72},{8,40},{44,76},{12,44},{48,8... | collective-permute-start | bytes 110600 | tf_op jit(solution)/shard_map/total/ppermute | solution.py:77
  14.9 0.0 collective-permute-start.1
  14.9 0.4 collective-permute-done.4
  15.3 0.2 collective-permute-done.3
  15.5 0.4 collective-permute-done.2
  16.0 0.2 collective-permute-done.1
  16.1 2.1 %collective-permute-start.8 = (bf16[48,384]{1,0:T(8,128)(2,1)S(1)}, bf16[48,384]{1,0:T(8,128)(2,1)S(1)}, u32[]{:S(2)}, u32[]{:S(2)}) collective-permute-start(bf16[48,384]{1,0:T(8,128)(2,1)S(1)} %add_convert_fusion.2), channel_id=1, source_target_pairs={{0,44},{32,0},{4,40},{36,4},{8,36},{40,8},{12,32},{44,12},{16,60},... | collective-permute-start | bytes 110600 | tf_op jit(solution)/shard_map/total/ppermute | solution.py:77
  18.3 2.7 %collective-permute-start.7 = (bf16[48,384]{1,0:T(8,128)(2,1)S(1)}, bf16[48,384]{1,0:T(8,128)(2,1)S(1)}, u32[]{:S(2)}, u32[]{:S(2)}) collective-permute-start(bf16[48,384]{1,0:T(8,128)(2,1)S(1)} %add_convert_fusion.2), channel_id=1, source_target_pairs={{0,40},{32,0},{4,44},{36,4},{8,32},{40,8},{12,36},{44,12},{16,56},... | collective-permute-start | bytes 110600 | tf_op jit(solution)/shard_map/total/ppermute | solution.py:77
  21.0 0.7 %collective-permute-start.6 = (bf16[48,384]{1,0:T(8,128)(2,1)S(1)}, bf16[48,384]{1,0:T(8,128)(2,1)S(1)}, u32[]{:S(2)}, u32[]{:S(2)}) collective-permute-start(bf16[48,384]{1,0:T(8,128)(2,1)S(1)} %add_convert_fusion.2), channel_id=1, source_target_pairs={{0,36},{32,0},{4,32},{36,4},{8,44},{40,8},{12,40},{44,12},{16,52},... | collective-permute-start | bytes 110600 | tf_op jit(solution)/shard_map/total/ppermute | solution.py:77
  21.6 0.0 collective-permute-start.5
  21.6 2.5 %collective-permute-done.8 = bf16[48,384]{1,0:T(8,128)(2,1)S(1)} collective-permute-done((bf16[48,384]{1,0:T(8,128)(2,1)S(1)}, bf16[48,384]{1,0:T(8,128)(2,1)S(1)}, u32[]{:S(2)}, u32[]{:S(2)}) %collective-permute-start.8) | collective-permute-done | bytes 36896 | tf_op jit(solution)/shard_map/total/ppermute | solution.py:77
  24.1 0.0 collective-permute-done.7
  24.1 0.7 %collective-permute-done.6 = bf16[48,384]{1,0:T(8,128)(2,1)S(1)} collective-permute-done((bf16[48,384]{1,0:T(8,128)(2,1)S(1)}, bf16[48,384]{1,0:T(8,128)(2,1)S(1)}, u32[]{:S(2)}, u32[]{:S(2)}) %collective-permute-start.6) | collective-permute-done | bytes 36896 | tf_op jit(solution)/shard_map/total/ppermute | solution.py:77
  24.8 0.0 collective-permute-done.5
  24.8 2.5 %collective-permute-start.12 = (bf16[48,384]{1,0:T(8,128)(2,1)S(1)}, bf16[48,384]{1,0:T(8,128)(2,1)S(1)}, u32[]{:S(2)}, u32[]{:S(2)}) collective-permute-start(bf16[48,384]{1,0:T(8,128)(2,1)S(1)} %add_convert_fusion.1), channel_id=1, source_target_pairs={{32,195},{0,32},{36,199},{4,36},{40,203},{8,40},{44,207},{12,44},{... | collective-permute-start | bytes 110600 | tf_op jit(solution)/shard_map/total/ppermute | solution.py:77
  27.4 0.0 collective-permute-start.11
  27.4 0.9 %collective-permute-start.10 = (bf16[48,384]{1,0:T(8,128)(2,1)S(1)}, bf16[48,384]{1,0:T(8,128)(2,1)S(1)}, u32[]{:S(2)}, u32[]{:S(2)}) collective-permute-start(bf16[48,384]{1,0:T(8,128)(2,1)S(1)} %add_convert_fusion.1), channel_id=1, source_target_pairs={{32,192},{0,32},{36,196},{4,36},{40,200},{8,40},{44,204},{12,44},{... | collective-permute-start | bytes 110600 | tf_op jit(solution)/shard_map/total/ppermute | solution.py:77
  28.3 0.0 collective-permute-start.9
  28.3 0.1 collective-permute-done.12
  28.4 0.2 collective-permute-done.11
  28.6 0.8 %collective-permute-done.10 = bf16[48,384]{1,0:T(8,128)(2,1)S(1)} collective-permute-done((bf16[48,384]{1,0:T(8,128)(2,1)S(1)}, bf16[48,384]{1,0:T(8,128)(2,1)S(1)}, u32[]{:S(2)}, u32[]{:S(2)}) %collective-permute-start.10) | collective-permute-done | bytes 36896 | tf_op jit(solution)/shard_map/total/ppermute | solution.py:77
  29.4 0.2 collective-permute-done.9
  29.6 3.0 %collective-permute-start.14 = (bf16[48,384]{1,0:T(8,128)(2,1)S(1)}, bf16[48,384]{1,0:T(8,128)(2,1)S(1)}, u32[]{:S(2)}, u32[]{:S(2)}) collective-permute-start(bf16[48,384]{1,0:T(8,128)(2,1)S(1)} %add_convert_fusion), channel_id=1, source_target_pairs={{0,60},{32,0},{4,56},{36,4},{8,52},{40,8},{12,48},{44,12},{16,44},... | collective-permute-start | bytes 110600 | tf_op jit(solution)/shard_map/total/ppermute | solution.py:77
  32.6 1.2 %collective-permute-start.13 = (bf16[48,384]{1,0:T(8,128)(2,1)S(1)}, bf16[48,384]{1,0:T(8,128)(2,1)S(1)}, u32[]{:S(2)}, u32[]{:S(2)}) collective-permute-start(bf16[48,384]{1,0:T(8,128)(2,1)S(1)} %add_convert_fusion), channel_id=1, source_target_pairs={{0,32},{32,0},{4,36},{36,4},{8,40},{40,8},{12,44},{44,12},{16,48},... | collective-permute-start | bytes 110600 | tf_op jit(solution)/shard_map/total/ppermute | solution.py:78
  33.8 3.8 %collective-permute-done.14 = bf16[48,384]{1,0:T(8,128)(2,1)S(1)} collective-permute-done((bf16[48,384]{1,0:T(8,128)(2,1)S(1)}, bf16[48,384]{1,0:T(8,128)(2,1)S(1)}, u32[]{:S(2)}, u32[]{:S(2)}) %collective-permute-start.14) | collective-permute-done | bytes 36896 | tf_op jit(solution)/shard_map/total/ppermute | solution.py:77
  37.6 0.0 collective-permute-done.13
  37.6 0.1 collective-permute-start.15
  37.7 0.0 copy-done.6
  37.7 0.1 copy.8.rate
  37.8 1.1 %collective-permute-done.15 = f32[48,384]{1,0:T(8,128)S(1)} collective-permute-done((f32[48,384]{1,0:T(8,128)S(1)}, f32[48,384]{1,0:T(8,128)S(1)}, u32[]{:S(2)}, u32[]{:S(2)}) %collective-permute-start.15) | collective-permute-done | bytes 73760 | tf_op jit(solution)/shard_map/total/ppermute | solution.py:85
  38.9 0.0 copy-done.1
  39.0 0.0 copy-done.5
  39.0 0.0 copy-start.2
  39.0 1.9 %copy-done.2 = bf16[8,768,144]{2,1,0:T(8,128)(2,1)S(1)} copy-done((bf16[8,768,144]{2,1,0:T(8,128)(2,1)S(1)}, bf16[8,768,144]{2,1,0:T(8,128)(2,1)}, u32[]{:S(2)}) %copy-start.2) | copy-done | bytes 1769496
  40.9 4.4 %synthesise.1 = (bf16[4,2,768,256]{3,2,1,0:T(8,128)(2,1)}, f32[4,2,48,48]{3,2,1,0:T(8,128)}) custom-call(f32[48,384]{1,0:T(8,128)S(1)} %broadcast_select_fusion.sums, f32[4,2,48,48]{3,2,1,0:T(8,128)S(1)} %copy-done.5, f32[4,2]{1,0:T(4,128)S(1)} %copy.8.rate, bf16[8,768,144]{2,1,0:T(8,128)(2,1)S(1)} %copy-done.2, bf16[32,96,256]{2,1,0:T(8,128)(2,1)S(1)} %copy-done.1), custom_call_target="tpu_custom_call" | custom-call | tf_op jit(solution)/shard_map/synthesise/pallas_call | solution.py:216
  (8 shorter events, 0.1 us)
Async XLA Ops:
  0.6 1.4 %copy-start = (bf16[32,96,256]{2,1,0:T(8,128)(2,1)S(1)}, bf16[32,96,256]{2,1,0:T(8,128)(2,1)}, u32[]{:S(2)}) copy-start(bf16[32,96,256]{2,1,0:T(8,128)(2,1)} %constant.15.clone.refs_2_.y_tables) | copy-start | bytes 4718596
  2.0 1.9 %copy-start.3 = (bf16[4,2,768,256]{3,2,1,0:T(8,128)(2,1)S(1)}, bf16[4,2,768,256]{3,2,1,0:T(8,128)(2,1)}, u32[]{:S(2)}) copy-start(bf16[4,2,768,256]{3,2,1,0:T(8,128)(2,1)} %refs_0_.1) | copy-start | bytes 9437188
  3.9 1.1 %copy-start.4 = (bf16[8,48,768]{2,1,0:T(8,128)(2,1)S(1)}, bf16[8,48,768]{2,1,0:T(8,128)(2,1)}, u32[]{:S(2)}) copy-start(bf16[8,48,768]{2,1,0:T(8,128)(2,1)} %constant.14.clone.refs_1_) | copy-start | bytes 1769476
  5.0 32.7 %copy-start.6 = (f32[4,2]{0,1:T(2,128)S(1)}, f32[4,2]{0,1:T(2,128)}, u32[]{:S(2)}) copy-start(f32[4,2]{0,1:T(2,128)} %param.8) | copy-start | bytes 100
  5.0 33.9 %copy-start.1 = (bf16[32,96,256]{2,1,0:T(8,128)(2,1)S(1)}, bf16[32,96,256]{2,1,0:T(8,128)(2,1)}, u32[]{:S(2)}) copy-start(bf16[32,96,256]{2,1,0:T(8,128)(2,1)} %constant.15.clone.refs_2_.y_tables) | copy-start | bytes 4718596
  5.0 34.0 %copy-start.5 = (f32[4,2,48,48]{3,2,1,0:T(8,128)S(1)}, f32[4,2,48,48]{3,2,1,0:T(8,128)}, u32[]{:S(2)}) copy-start(f32[4,2,48,48]{3,2,1,0:T(8,128)} %parent.1) | copy-start | bytes 221188
  9.3 4.2 %collective-permute-start = (bf16[48,384]{1,0:T(8,128)(2,1)S(1)}, bf16[48,384]{1,0:T(8,128)(2,1)S(1)}, u32[]{:S(2)}, u32[]{:S(2)}) collective-permute-start(bf16[48,384]{1,0:T(8,128)(2,1)S(1)} %convert_element_type.63), channel_id=1, source_target_pairs={{0,32},{32,0},{4,36},{36,4},{8,40},{40,8},{12,44},{44,12},{16,48},... | collective-permute-start | bytes 110600 | tf_op jit(solution)/shard_map/total/ppermute | solution.py:73
  13.5 1.9 %collective-permute-start.4 = (bf16[48,384]{1,0:T(8,128)(2,1)S(1)}, bf16[48,384]{1,0:T(8,128)(2,1)S(1)}, u32[]{:S(2)}, u32[]{:S(2)}) collective-permute-start(bf16[48,384]{1,0:T(8,128)(2,1)S(1)} %add_convert_fusion.3), channel_id=1, source_target_pairs={{32,65},{0,32},{36,69},{4,36},{40,73},{8,40},{44,77},{12,44},{48,8... | collective-permute-start | bytes 110600 | tf_op jit(solution)/shard_map/total/ppermute | solution.py:77
  14.3 1.3 %collective-permute-start.3 = (bf16[48,384]{1,0:T(8,128)(2,1)S(1)}, bf16[48,384]{1,0:T(8,128)(2,1)S(1)}, u32[]{:S(2)}, u32[]{:S(2)}) collective-permute-start(bf16[48,384]{1,0:T(8,128)(2,1)S(1)} %add_convert_fusion.3), channel_id=1, source_target_pairs={{32,1},{0,32},{36,5},{4,36},{40,9},{8,40},{44,13},{12,44},{48,17},... | collective-permute-start | bytes 110600 | tf_op jit(solution)/shard_map/total/ppermute | solution.py:77
  14.3 1.7 %collective-permute-start.2 = (bf16[48,384]{1,0:T(8,128)(2,1)S(1)}, bf16[48,384]{1,0:T(8,128)(2,1)S(1)}, u32[]{:S(2)}, u32[]{:S(2)}) collective-permute-start(bf16[48,384]{1,0:T(8,128)(2,1)S(1)} %add_convert_fusion.3), channel_id=1, source_target_pairs={{32,64},{0,32},{36,68},{4,36},{40,72},{8,40},{44,76},{12,44},{48,8... | collective-permute-start | bytes 110600 | tf_op jit(solution)/shard_map/total/ppermute | solution.py:77
  14.9 1.2 %collective-permute-start.1 = (bf16[48,384]{1,0:T(8,128)(2,1)S(1)}, bf16[48,384]{1,0:T(8,128)(2,1)S(1)}, u32[]{:S(2)}, u32[]{:S(2)}) collective-permute-start(bf16[48,384]{1,0:T(8,128)(2,1)S(1)} %add_convert_fusion.3), channel_id=1, source_target_pairs={{0,32},{32,0},{4,36},{36,4},{8,40},{40,8},{12,44},{44,12},{16,48},... | collective-permute-start | bytes 110600 | tf_op jit(solution)/shard_map/total/ppermute | solution.py:78
  16.1 8.0 %collective-permute-start.8 = (bf16[48,384]{1,0:T(8,128)(2,1)S(1)}, bf16[48,384]{1,0:T(8,128)(2,1)S(1)}, u32[]{:S(2)}, u32[]{:S(2)}) collective-permute-start(bf16[48,384]{1,0:T(8,128)(2,1)S(1)} %add_convert_fusion.2), channel_id=1, source_target_pairs={{0,44},{32,0},{4,40},{36,4},{8,36},{40,8},{12,32},{44,12},{16,60},... | collective-permute-start | bytes 110600 | tf_op jit(solution)/shard_map/total/ppermute | solution.py:77
  18.3 5.8 %collective-permute-start.7 = (bf16[48,384]{1,0:T(8,128)(2,1)S(1)}, bf16[48,384]{1,0:T(8,128)(2,1)S(1)}, u32[]{:S(2)}, u32[]{:S(2)}) collective-permute-start(bf16[48,384]{1,0:T(8,128)(2,1)S(1)} %add_convert_fusion.2), channel_id=1, source_target_pairs={{0,40},{32,0},{4,44},{36,4},{8,32},{40,8},{12,36},{44,12},{16,56},... | collective-permute-start | bytes 110600 | tf_op jit(solution)/shard_map/total/ppermute | solution.py:77
  21.0 3.8 %collective-permute-start.6 = (bf16[48,384]{1,0:T(8,128)(2,1)S(1)}, bf16[48,384]{1,0:T(8,128)(2,1)S(1)}, u32[]{:S(2)}, u32[]{:S(2)}) collective-permute-start(bf16[48,384]{1,0:T(8,128)(2,1)S(1)} %add_convert_fusion.2), channel_id=1, source_target_pairs={{0,36},{32,0},{4,32},{36,4},{8,44},{40,8},{12,40},{44,12},{16,52},... | collective-permute-start | bytes 110600 | tf_op jit(solution)/shard_map/total/ppermute | solution.py:77
  21.6 3.2 %collective-permute-start.5 = (bf16[48,384]{1,0:T(8,128)(2,1)S(1)}, bf16[48,384]{1,0:T(8,128)(2,1)S(1)}, u32[]{:S(2)}, u32[]{:S(2)}) collective-permute-start(bf16[48,384]{1,0:T(8,128)(2,1)S(1)} %add_convert_fusion.2), channel_id=1, source_target_pairs={{0,32},{32,0},{4,36},{36,4},{8,40},{40,8},{12,44},{44,12},{16,48},... | collective-permute-start | bytes 110600 | tf_op jit(solution)/shard_map/total/ppermute | solution.py:78
  24.8 3.6 %collective-permute-start.12 = (bf16[48,384]{1,0:T(8,128)(2,1)S(1)}, bf16[48,384]{1,0:T(8,128)(2,1)S(1)}, u32[]{:S(2)}, u32[]{:S(2)}) collective-permute-start(bf16[48,384]{1,0:T(8,128)(2,1)S(1)} %add_convert_fusion.1), channel_id=1, source_target_pairs={{32,195},{0,32},{36,199},{4,36},{40,203},{8,40},{44,207},{12,44},{... | collective-permute-start | bytes 110600 | tf_op jit(solution)/shard_map/total/ppermute | solution.py:77
  27.4 1.2 %collective-permute-start.11 = (bf16[48,384]{1,0:T(8,128)(2,1)S(1)}, bf16[48,384]{1,0:T(8,128)(2,1)S(1)}, u32[]{:S(2)}, u32[]{:S(2)}) collective-permute-start(bf16[48,384]{1,0:T(8,128)(2,1)S(1)} %add_convert_fusion.1), channel_id=1, source_target_pairs={{32,3},{0,32},{36,7},{4,36},{40,11},{8,40},{44,15},{12,44},{48,19}... | collective-permute-start | bytes 110600 | tf_op jit(solution)/shard_map/total/ppermute | solution.py:77
  27.4 2.0 %collective-permute-start.10 = (bf16[48,384]{1,0:T(8,128)(2,1)S(1)}, bf16[48,384]{1,0:T(8,128)(2,1)S(1)}, u32[]{:S(2)}, u32[]{:S(2)}) collective-permute-start(bf16[48,384]{1,0:T(8,128)(2,1)S(1)} %add_convert_fusion.1), channel_id=1, source_target_pairs={{32,192},{0,32},{36,196},{4,36},{40,200},{8,40},{44,204},{12,44},{... | collective-permute-start | bytes 110600 | tf_op jit(solution)/shard_map/total/ppermute | solution.py:77
  28.3 1.2 %collective-permute-start.9 = (bf16[48,384]{1,0:T(8,128)(2,1)S(1)}, bf16[48,384]{1,0:T(8,128)(2,1)S(1)}, u32[]{:S(2)}, u32[]{:S(2)}) collective-permute-start(bf16[48,384]{1,0:T(8,128)(2,1)S(1)} %add_convert_fusion.1), channel_id=1, source_target_pairs={{0,32},{32,0},{4,36},{36,4},{8,40},{40,8},{12,44},{44,12},{16,48},... | collective-permute-start | bytes 110600 | tf_op jit(solution)/shard_map/total/ppermute | solution.py:78
  29.6 8.0 %collective-permute-start.14 = (bf16[48,384]{1,0:T(8,128)(2,1)S(1)}, bf16[48,384]{1,0:T(8,128)(2,1)S(1)}, u32[]{:S(2)}, u32[]{:S(2)}) collective-permute-start(bf16[48,384]{1,0:T(8,128)(2,1)S(1)} %add_convert_fusion), channel_id=1, source_target_pairs={{0,60},{32,0},{4,56},{36,4},{8,52},{40,8},{12,48},{44,12},{16,44},... | collective-permute-start | bytes 110600 | tf_op jit(solution)/shard_map/total/ppermute | solution.py:77
  32.6 5.0 %collective-permute-start.13 = (bf16[48,384]{1,0:T(8,128)(2,1)S(1)}, bf16[48,384]{1,0:T(8,128)(2,1)S(1)}, u32[]{:S(2)}, u32[]{:S(2)}) collective-permute-start(bf16[48,384]{1,0:T(8,128)(2,1)S(1)} %add_convert_fusion), channel_id=1, source_target_pairs={{0,32},{32,0},{4,36},{36,4},{8,40},{40,8},{12,44},{44,12},{16,48},... | collective-permute-start | bytes 110600 | tf_op jit(solution)/shard_map/total/ppermute | solution.py:78
  37.6 1.4 %collective-permute-start.15 = (f32[48,384]{1,0:T(8,128)S(1)}, f32[48,384]{1,0:T(8,128)S(1)}, u32[]{:S(2)}, u32[]{:S(2)}) collective-permute-start(f32[48,384]{1,0:T(8,128)S(1)} %convert_add_fusion), channel_id=1, source_target_pairs={{0,32},{32,0},{4,36},{36,4},{8,40},{40,8},{12,44},{44,12},{16,48},... | collective-permute-start | bytes 221192 | tf_op jit(solution)/shard_map/total/ppermute | solution.py:85
  39.0 1.9 %copy-start.2 = (bf16[8,768,144]{2,1,0:T(8,128)(2,1)S(1)}, bf16[8,768,144]{2,1,0:T(8,128)(2,1)}, u32[]{:S(2)}) copy-start(bf16[8,768,144]{2,1,0:T(8,128)(2,1)} %constant.16.clone.x_tables) | copy-start | bytes 5308420

commit v2 on v1

--- a/solution.py
+++ b/solution.py
@@ -64,26 +64,37 @@
 FLIP_Z0 = lambda x, y, z: (x, y, z ^ 1)
 FLIP_Z1 = lambda x, y, z: (x, y, z ^ 2)
 FLIP_Z2 = lambda x, y, z: (x, y, 7 - z)
-STAGES = ((FLIP_X0, FLIP_Y0), (FLIP_Z0, FLIP_Z1), (FLIP_X1, FLIP_Y1), (FLIP_Z2,))
-
-
-def total_of(partial):
-    core = 1
-    half = partial.astype(jnp.bfloat16)
+STAGES = ((FLIP_X1, FLIP_Y1), (FLIP_Z1, FLIP_Z2), (FLIP_Y0, FLIP_Z0))
+LAST = FLIP_X0
+
+
+def on_both(move):
+    pairs = []
+    for x, y, z in CHIPS:
+        to_x, to_y, to_z = move(x, y, z)
+        pairs += [(index_of(x, c, z, y), index_of(to_x, c, to_z, to_y)) for c in (0, 1)]
+    return pairs
+
+
+def total_of(half):
+    core = 0
     running = half.astype(jnp.float32) + lax.ppermute(half, AXES, swap_cores()).astype(jnp.float32)
     for stage in STAGES:
         value = running.astype(jnp.bfloat16)
-        moves = stage if len(stage) == 1 else (*stage, both(*stage))
-        near = [lax.ppermute(value, AXES, hand_over(core, move)) for move in moves]
+        near = [
+            lax.ppermute(value, AXES, hand_over(core, move)).astype(jnp.float32)
+            for move in (*stage, both(*stage))
+        ]
         own = lax.ppermute(value, AXES, swap_cores()).astype(jnp.float32)
-        near = [part.astype(jnp.float32) for part in near]
-        if len(near) == 1:
-            running = own + near[0]
-        else:
-            running = (own + near[0]) + (near[1] + near[2])
+        running = (own + near[0]) + (near[1] + near[2])
         core = 1 - core
-    other = lax.ppermute(running, AXES, swap_cores())
-    return jnp.where(lax.axis_index("c") == core, running, other)
+    value = running.astype(jnp.bfloat16)
+    crossed = lax.ppermute(value, AXES, hand_over(core, LAST))
+    straight = lax.ppermute(value, AXES, on_both(LAST))
+    own = lax.ppermute(value, AXES, swap_cores())
+    holds = lax.axis_index("c") == core
+    own = jnp.where(holds, value, own).astype(jnp.float32)
+    return own + jnp.where(holds, straight, crossed).astype(jnp.float32)
 
 
 def mask_of(flat, rows):
@@ -106,31 +117,36 @@
     return gx, gy
 
 
-def analyse(scale, fields, x_tables, y_tables, out, blocks, x_table, y_table, high, low, sems):
+def analyse(
+    scale, fields, x_tables, y_tables, x_wides, out, x_wide, y_table, blocks, x_table, high, low, sems
+):
     gx, gy = where_am_i()
-    copy_y = pltpu.make_async_copy(y_tables.at[gy], y_table, sems.at[FLAT])
-    copy_x = pltpu.make_async_copy(x_tables.at[gx], x_table, sems.at[FLAT + 1])
+    copy_y = pltpu.make_async_copy(y_tables.at[gy, pl.ds(0, 2 * MODES)], y_table, sems.at[FLAT])
+    copy_x = pltpu.make_async_copy(x_tables.at[gx, pl.ds(0, MODES)], x_table, sems.at[FLAT + 1])
+    copy_wide = pltpu.make_async_copy(x_wides.at[gx], x_wide, sems.at[FLAT + 2])
     copies = [
         pltpu.make_async_copy(fields.at[f // 2, f % 2], blocks.at[f], sems.at[f])
         for f in range(FLAT)
     ]
+    copies[0].start()
     copy_x.start()
-    copies[0].start()
     copy_y.start()
     for copy in copies[1:]:
         copy.start()
-    copy_x.wait()
-    for f in range(FLAT):
-        copies[f].wait()
-        high[pl.ds(f * MODES, MODES)], low[pl.ds(f * MODES, MODES)] = split(
-            dot(x_table[...], blocks[f])
-        )
+    copy_wide.start()
     copy_y.wait()
     row = lax.broadcasted_iota(jnp.int32, (WIDTH, MODES), 0)
     mode = lax.broadcasted_iota(jnp.int32, (WIDTH, MODES), 1)
     spread = (row // 128 * PIECE + row % PIECE == mode).astype(jnp.bfloat16)
     y_high = dot(spread, y_table[:MODES]).astype(jnp.bfloat16)
     y_low = dot(spread, y_table[MODES:]).astype(jnp.bfloat16)
+    copy_x.wait()
+    for pair in range(0, FLAT, 2):
+        copies[pair].wait()
+        copies[pair + 1].wait()
+        for f in (pair, pair + 1):
+            mine = pl.ds(f * MODES, MODES)
+            high[mine], low[mine] = split(dot(x_table[...], blocks[f]))
     last = ((1,), (1,))
     product = (
         dot(high[...], y_high, last) + dot(low[...], y_high, last) + dot(high[...], y_low, last)
@@ -138,15 +154,11 @@
     total = jnp.zeros((MODES, WIDTH), jnp.float32)
     for f in range(FLAT):
         total = jnp.where(mask_of(f, MODES), product[f * MODES : (f + 1) * MODES], total)
-    out[...] = total * scale
-
-
-def synthesise(sums, parent, rate, x_tables, y_tables, out, spectra, blocks, x_table, y_table, sems):
-    gx, gy = where_am_i()
-    copy_y = pltpu.make_async_copy(y_tables.at[gy], y_table, sems.at[FLAT])
-    copy_x = pltpu.make_async_copy(x_tables.at[gx], x_table, sems.at[FLAT + 1])
-    copy_y.start()
-    copy_x.start()
+    out[...] = (total * scale).astype(jnp.bfloat16)
+    copy_wide.wait()
+
+
+def synthesise(sums, parent, rate, x_table, y_table, out, spectra, blocks, sems):
     high, low = split(sums[...])
     none = jnp.zeros((MODES, WIDTH), jnp.bfloat16)
     highs = jnp.concatenate([jnp.where(mask_of(f, MODES), high, none) for f in range(FLAT)])
@@ -155,7 +167,6 @@
     mode = lax.broadcasted_iota(jnp.int32, (WIDTH, MODES), 1)
     gather = (row // 128 * PIECE + row % PIECE == mode).astype(jnp.bfloat16)
     coeffs = dot(highs, gather) + dot(lows, gather)
-    copy_y.wait()
     y_high, y_low = y_table[:MODES], y_table[MODES:]
     rows = []
     for f in range(FLAT):
@@ -165,7 +176,6 @@
     d_high, d_low = split(jnp.concatenate(rows))
     across = dot(d_high, y_high) + dot(d_low, y_high) + dot(d_high, y_low)
     a_high, a_low = split(across)
-    copy_x.wait()
     copies = []
     for f in range(FLAT):
         mine = slice(f * MODES, (f + 1) * MODES)
@@ -184,53 +194,54 @@
     cols_x, cols_y = total_x // 8, total_y // 32
     x_high, x_low = halves(basis(total_x))
     y_high, y_low = halves(basis(total_y))
-    narrow = x_high.reshape(8, cols_x, MODES).transpose(0, 2, 1)
-    x_tables = np.concatenate([x_high, x_low, x_high], 1).reshape(8, cols_x, 3 * MODES)
+    narrow = np.pad(x_high.reshape(8, cols_x, MODES).transpose(0, 2, 1), ((0, 0), (0, 208), (0, 0)))
+    x_wides = np.concatenate([x_high, x_low, x_high], 1).reshape(8, cols_x, 3 * MODES)
     y_tables = np.concatenate(
         [t.reshape(32, cols_y, MODES).transpose(0, 2, 1) for t in (y_high, y_low)], 1
     )
+    y_tables = np.pad(y_tables, ((0, 0), (0, 96), (0, 0)))
     scale = 2.0 / math.sqrt(total_x * total_y)
     any_space = pl.BlockSpec(memory_space=pl.ANY)
     vmem = pl.BlockSpec(memory_space=pltpu.VMEM)
-    grant = pltpu.CompilerParams(vmem_limit_bytes=24 * 1024 * 1024)
+    small = jax.ShapeDtypeStruct((MODES, WIDTH), jnp.bfloat16)
 
     def per_device(fields, parent, rate):
-        partial = pl.pallas_call(
+        partial, x_wide, y_table = pl.pallas_call(
             lambda *refs: analyse(scale, *refs),
-            out_shape=jax.ShapeDtypeStruct((MODES, WIDTH), jnp.float32),
-            in_specs=[any_space] * 3,
-            out_specs=vmem,
+            out_shape=(
+                small,
+                jax.ShapeDtypeStruct((cols_x, 3 * MODES), jnp.bfloat16),
+                jax.ShapeDtypeStruct((2 * MODES, cols_y), jnp.bfloat16),
+            ),
+            in_specs=[any_space] * 4,
+            out_specs=(vmem, vmem, vmem),
             scratch_shapes=[
                 pltpu.VMEM((FLAT, cols_x, cols_y), jnp.bfloat16),
                 pltpu.VMEM((MODES, cols_x), jnp.bfloat16),
-                pltpu.VMEM((2 * MODES, cols_y), jnp.bfloat16),
                 pltpu.VMEM((FLAT * MODES, cols_y), jnp.bfloat16),
                 pltpu.VMEM((FLAT * MODES, cols_y), jnp.bfloat16),
-                pltpu.SemaphoreType.DMA((FLAT + 2,)),
+                pltpu.SemaphoreType.DMA((FLAT + 3,)),
             ],
-            compiler_params=grant,
+            compiler_params=pltpu.CompilerParams(vmem_limit_bytes=52 << 20),
             name="analyse",
-        )(fields, jnp.asarray(narrow), jnp.asarray(y_tables))
+        )(fields, jnp.asarray(narrow), jnp.asarray(y_tables), jnp.asarray(x_wides))
         with jax.named_scope("total"):
             sums = total_of(partial)
-        tendency, spectra = pl.pallas_call(
+        return pl.pallas_call(
             synthesise,
             out_shape=(
                 jax.ShapeDtypeStruct((4, 2, cols_x, cols_y), jnp.bfloat16),
                 jax.ShapeDtypeStruct((4, 2, MODES, MODES), jnp.float32),
             ),
-            in_specs=[vmem, vmem, pl.BlockSpec(memory_space=pltpu.SMEM), any_space, any_space],
+            in_specs=[vmem, vmem, pl.BlockSpec(memory_space=pltpu.SMEM), vmem, vmem],
             out_specs=(any_space, vmem),
             scratch_shapes=[
                 pltpu.VMEM((FLAT, cols_x, cols_y), jnp.bfloat16),
-                pltpu.VMEM((cols_x, 3 * MODES), jnp.bfloat16),
-                pltpu.VMEM((2 * MODES, cols_y), jnp.bfloat16),
-                pltpu.SemaphoreType.DMA((FLAT + 2,)),
+                pltpu.SemaphoreType.DMA((FLAT,)),
             ],
-            compiler_params=grant,
+            compiler_params=pltpu.CompilerParams(vmem_limit_bytes=16 << 20),
             name="synthesise",
-        )(sums, parent, rate, jnp.asarray(x_tables), jnp.asarray(y_tables))
-        return tendency, spectra
+        )(sums, parent, rate, x_wide, y_table)
 
     grid = P(None, None, ("x", "c"), ("z", "y"))
     return jax.shard_map(

time: 45.5 us -> 37 us (0.81)
  local copies, waits for them, and re-layouts: 6.35 us -> 0.1 us
  Pallas kernels: 8.62 us -> 6.72 us
  waiting for transfers between devices: 11.4 us -> 10.8 us
    unnamed x15 -> x5, local copies, waits for them, and re-layouts: 6.35 us -> 0.1 us
    pallas_call x1, Pallas kernels: 4.23 us -> 2.75 us  [per_device(): pl.pallas_call(lambda *refs: analyse(scale, *refs), out_shape=(small, jax...]
    ppermute x11 -> x12, waiting for transfers between devices: 10.2 us -> 9.87 us  [the longest x9 7.57 us: total_of(): lax.ppermute(value, AXES, hand_over(core, move)).astype(jnp.float32)]
    ppermute x11 -> x12, starting transfers between devices: 13.5 us -> 13.8 us  [the longest x9 13.2 us: total_of(): lax.ppermute(value, AXES, hand_over(core, move)).astype(jnp.float32)]
    ppermute x4 -> x3, starting transfers between devices: 1.2 us -> 1.29 us  [total_of(): own = lax.ppermute(value, AXES, swap_cores()).astype(jnp.float32)]
  transfers between devices with their start and end apart: 16 -> 16, of which waited for: 13 -> 11; matrix products, arithmetic and copies ran while one was open for 0% -> 0% of each run, Pallas kernels for 0% -> 0%
where the time goes in v2:
time: 37 us; the launch traced here: 36.9 us
  starting transfers between devices  18.4 us (50%)
  waiting for transfers between devices  10.8 us (29%)
  Pallas kernels  6.72 us (18%)
  between operations  0.7 us (2%)
    ppermute x9, starting transfers between devices, total_of(): lax.ppermute(value, AXES, hand_over(core, move)).astype(jnp.float32)  13.2 us
    ppermute x9, waiting for transfers between devices, total_of(): lax.ppermute(value, AXES, hand_over(core, move)).astype(jnp.float32)  7.57 us
    pallas_call x1, Pallas kernels, per_device(): pl.pallas_call(synthesise, out_shape=(jax.ShapeDtypeStruct((4, 2, cols_x,...  3.96 us
    ppermute x1, starting transfers between devices, total_of(): lax.ppermute(half, AXES, swap_cores()).astype(jnp.float32)  3.33 us
    pallas_call x1, Pallas kernels, per_device(): pl.pallas_call(lambda *refs: analyse(scale, *refs), out_shape=(small, jax...  2.75 us
    ppermute x1, waiting for transfers between devices, total_of(): straight = lax.ppermute(value, AXES, on_both(LAST))  1.7 us
    ppermute x3, starting transfers between devices, total_of(): own = lax.ppermute(value, AXES, swap_cores()).astype(jnp.float32)  1.29 us
    ppermute x1, waiting for transfers between devices, total_of(): lax.ppermute(half, AXES, swap_cores()).astype(jnp.float32)  0.87 us
  transfers between devices with their start and end apart: 16, of which 11 were waited for; matrix products, arithmetic and copies ran while one was open for 0% of the time, Pallas kernels for 0%

profile of v2, /device:TPU:1, one launch (start us, length us, event | category | flops | bytes accessed | tf_op | source)
XLA Modules:
  0.0 36.9 jit_solution(12516902999419087794)
XLA Ops:
  0.6 0.0 copy-start.1
  0.6 0.0 copy-start
  0.6 2.8 %analyse.1 = (bf16[48,384]{1,0:T(8,128)(2,1)S(1)}, bf16[768,144]{1,0:T(8,128)(2,1)S(1)}, bf16[96,256]{1,0:T(8,128)(2,1)S(1)}) custom-call(bf16[4,2,768,256]{3,2,1,0:T(8,128)(2,1)} %refs_0_.1, bf16[8,256,768]{2,1,0:T(8,128)(2,1)} %constant.14.clone.refs_1_, bf16[32,192,256]{2,1,0:T(8,128)(2,1)} %constant.15.clone.refs_2_, ...), custom_call_target="tpu_custom_call" | custom-call | tf_op jit(solution)/shard_map/analyse/pallas_call | solution.py:209
  3.4 3.3 %collective-permute-start = (bf16[48,384]{1,0:T(8,128)(2,1)S(1)}, bf16[48,384]{1,0:T(8,128)(2,1)S(1)}, u32[]{:S(2)}, u32[]{:S(2)}) collective-permute-start(bf16[48,384]{1,0:T(8,128)(2,1)S(1)} %get-tuple-element.5), channel_id=1, source_target_pairs={{0,32},{32,0},{4,36},{36,4},{8,40},{40,8},{12,44},{44,12},{16,48},... | collective-permute-start | bytes 110600 | tf_op jit(solution)/shard_map/total/ppermute | solution.py:81
  6.7 0.9 %collective-permute-done = bf16[48,384]{1,0:T(8,128)(2,1)S(1)} collective-permute-done((bf16[48,384]{1,0:T(8,128)(2,1)S(1)}, bf16[48,384]{1,0:T(8,128)(2,1)S(1)}, u32[]{:S(2)}, u32[]{:S(2)}) %collective-permute-start) | collective-permute-done | bytes 36896 | tf_op jit(solution)/shard_map/total/ppermute | solution.py:81
  7.6 0.4 %collective-permute-start.4 = (bf16[48,384]{1,0:T(8,128)(2,1)S(1)}, bf16[48,384]{1,0:T(8,128)(2,1)S(1)}, u32[]{:S(2)}, u32[]{:S(2)}) collective-permute-start(bf16[48,384]{1,0:T(8,128)(2,1)S(1)} %add_convert_fusion.3), channel_id=1, source_target_pairs={{0,227},{32,0},{4,231},{36,4},{8,235},{40,8},{12,239},{44,12},{16,... | collective-permute-start | bytes 110600 | tf_op jit(solution)/shard_map/total/ppermute | solution.py:85
  8.0 3.2 %collective-permute-start.3 = (bf16[48,384]{1,0:T(8,128)(2,1)S(1)}, bf16[48,384]{1,0:T(8,128)(2,1)S(1)}, u32[]{:S(2)}, u32[]{:S(2)}) collective-permute-start(bf16[48,384]{1,0:T(8,128)(2,1)S(1)} %add_convert_fusion.3), channel_id=1, source_target_pairs={{0,35},{32,0},{4,39},{36,4},{8,43},{40,8},{12,47},{44,12},{16,51},... | collective-permute-start | bytes 110600 | tf_op jit(solution)/shard_map/total/ppermute | solution.py:85
  11.3 0.0 collective-permute-start.2
  11.3 0.6 %collective-permute-start.1 = (bf16[48,384]{1,0:T(8,128)(2,1)S(1)}, bf16[48,384]{1,0:T(8,128)(2,1)S(1)}, u32[]{:S(2)}, u32[]{:S(2)}) collective-permute-start(bf16[48,384]{1,0:T(8,128)(2,1)S(1)} %add_convert_fusion.3), channel_id=1, source_target_pairs={{0,32},{32,0},{4,36},{36,4},{8,40},{40,8},{12,44},{44,12},{16,48},... | collective-permute-start | bytes 110600 | tf_op jit(solution)/shard_map/total/ppermute | solution.py:88
  11.9 2.5 %collective-permute-done.4 = bf16[48,384]{1,0:T(8,128)(2,1)S(1)} collective-permute-done((bf16[48,384]{1,0:T(8,128)(2,1)S(1)}, bf16[48,384]{1,0:T(8,128)(2,1)S(1)}, u32[]{:S(2)}, u32[]{:S(2)}) %collective-permute-start.4) | collective-permute-done | bytes 36896 | tf_op jit(solution)/shard_map/total/ppermute | solution.py:85
  14.4 0.0 collective-permute-done.3
  14.4 1.5 %collective-permute-done.2 = bf16[48,384]{1,0:T(8,128)(2,1)S(1)} collective-permute-done((bf16[48,384]{1,0:T(8,128)(2,1)S(1)}, bf16[48,384]{1,0:T(8,128)(2,1)S(1)}, u32[]{:S(2)}, u32[]{:S(2)}) %collective-permute-start.2) | collective-permute-done | bytes 36896 | tf_op jit(solution)/shard_map/total/ppermute | solution.py:85
  15.9 0.0 collective-permute-done.1
  15.9 4.1 %collective-permute-start.8 = (bf16[48,384]{1,0:T(8,128)(2,1)S(1)}, bf16[48,384]{1,0:T(8,128)(2,1)S(1)}, u32[]{:S(2)}, u32[]{:S(2)}) collective-permute-start(bf16[48,384]{1,0:T(8,128)(2,1)S(1)} %add_convert_fusion.2), channel_id=1, source_target_pairs={{32,20},{0,32},{36,16},{4,36},{40,28},{8,40},{44,24},{12,44},{48,4... | collective-permute-start | bytes 110600 | tf_op jit(solution)/shard_map/total/ppermute | solution.py:85
  20.0 2.0 %collective-permute-start.7 = (bf16[48,384]{1,0:T(8,128)(2,1)S(1)}, bf16[48,384]{1,0:T(8,128)(2,1)S(1)}, u32[]{:S(2)}, u32[]{:S(2)}) collective-permute-start(bf16[48,384]{1,0:T(8,128)(2,1)S(1)} %add_convert_fusion.2), channel_id=1, source_target_pairs={{32,28},{0,32},{36,24},{4,36},{40,20},{8,40},{44,16},{12,44},{48,1... | collective-permute-start | bytes 110600 | tf_op jit(solution)/shard_map/total/ppermute | solution.py:85
  22.0 0.0 collective-permute-start.6
  22.0 0.5 %collective-permute-start.5 = (bf16[48,384]{1,0:T(8,128)(2,1)S(1)}, bf16[48,384]{1,0:T(8,128)(2,1)S(1)}, u32[]{:S(2)}, u32[]{:S(2)}) collective-permute-start(bf16[48,384]{1,0:T(8,128)(2,1)S(1)} %add_convert_fusion.2), channel_id=1, source_target_pairs={{0,32},{32,0},{4,36},{36,4},{8,40},{40,8},{12,44},{44,12},{16,48},... | collective-permute-start | bytes 110600 | tf_op jit(solution)/shard_map/total/ppermute | solution.py:88
  22.5 0.0 collective-permute-done.8
  22.5 0.5 %collective-permute-done.7 = bf16[48,384]{1,0:T(8,128)(2,1)S(1)} collective-permute-done((bf16[48,384]{1,0:T(8,128)(2,1)S(1)}, bf16[48,384]{1,0:T(8,128)(2,1)S(1)}, u32[]{:S(2)}, u32[]{:S(2)}) %collective-permute-start.7) | collective-permute-done | bytes 36896 | tf_op jit(solution)/shard_map/total/ppermute | solution.py:85
  23.0 0.2 collective-permute-done.6
  23.2 0.1 collective-permute-done.5
  23.4 3.0 %collective-permute-start.12 = (bf16[48,384]{1,0:T(8,128)(2,1)S(1)}, bf16[48,384]{1,0:T(8,128)(2,1)S(1)}, u32[]{:S(2)}, u32[]{:S(2)}) collective-permute-start(bf16[48,384]{1,0:T(8,128)(2,1)S(1)} %add_convert_fusion.1), channel_id=1, source_target_pairs={{0,37},{32,0},{4,33},{36,4},{8,45},{40,8},{12,41},{44,12},{16,53},... | collective-permute-start | bytes 110600 | tf_op jit(solution)/shard_map/total/ppermute | solution.py:85
  26.4 0.1 collective-permute-start.11
  26.5 0.4 %collective-permute-start.10 = (bf16[48,384]{1,0:T(8,128)(2,1)S(1)}, bf16[48,384]{1,0:T(8,128)(2,1)S(1)}, u32[]{:S(2)}, u32[]{:S(2)}) collective-permute-start(bf16[48,384]{1,0:T(8,128)(2,1)S(1)} %add_convert_fusion.1), channel_id=1, source_target_pairs={{0,33},{32,0},{4,37},{36,4},{8,41},{40,8},{12,45},{44,12},{16,49},... | collective-permute-start | bytes 110600 | tf_op jit(solution)/shard_map/total/ppermute | solution.py:85
  26.8 0.2 collective-permute-start.9
  27.0 0.7 %collective-permute-done.12 = bf16[48,384]{1,0:T(8,128)(2,1)S(1)} collective-permute-done((bf16[48,384]{1,0:T(8,128)(2,1)S(1)}, bf16[48,384]{1,0:T(8,128)(2,1)S(1)}, u32[]{:S(2)}, u32[]{:S(2)}) %collective-permute-start.12) | collective-permute-done | bytes 36896 | tf_op jit(solution)/shard_map/total/ppermute | solution.py:85
  27.7 2.0 %collective-permute-done.11 = bf16[48,384]{1,0:T(8,128)(2,1)S(1)} collective-permute-done((bf16[48,384]{1,0:T(8,128)(2,1)S(1)}, bf16[48,384]{1,0:T(8,128)(2,1)S(1)}, u32[]{:S(2)}, u32[]{:S(2)}) %collective-permute-start.11) | collective-permute-done | bytes 36896 | tf_op jit(solution)/shard_map/total/ppermute | solution.py:85
  29.8 0.1 collective-permute-done.10
  29.9 0.0 collective-permute-done.9
  29.9 0.1 collective-permute-start.15
  30.0 0.2 collective-permute-start.14
  30.1 0.3 collective-permute-start.13
  30.5 0.0 copy-done.1
  30.5 0.1 copy.8.rate
  30.6 0.6 %collective-permute-done.15 = bf16[48,384]{1,0:T(8,128)(2,1)S(1)} collective-permute-done((bf16[48,384]{1,0:T(8,128)(2,1)S(1)}, bf16[48,384]{1,0:T(8,128)(2,1)S(1)}, u32[]{:S(2)}, u32[]{:S(2)}) %collective-permute-start.15) | collective-permute-done | bytes 36896 | tf_op jit(solution)/shard_map/total/ppermute | solution.py:92
  31.2 1.7 %collective-permute-done.14 = bf16[48,384]{1,0:T(8,128)(2,1)S(1)} collective-permute-done((bf16[48,384]{1,0:T(8,128)(2,1)S(1)}, bf16[48,384]{1,0:T(8,128)(2,1)S(1)}, u32[]{:S(2)}, u32[]{:S(2)}) %collective-permute-start.14) | collective-permute-done | bytes 36896 | tf_op jit(solution)/shard_map/total/ppermute | solution.py:93
  32.9 0.0 collective-permute-done.13
  32.9 0.0 copy-done
  32.9 4.0 %synthesise.1 = (bf16[4,2,768,256]{3,2,1,0:T(8,128)(2,1)}, f32[4,2,48,48]{3,2,1,0:T(8,128)}) custom-call(f32[48,384]{1,0:T(8,128)S(1)} %convert_add_fusion.sums, f32[4,2,48,48]{3,2,1,0:T(8,128)S(1)} %copy-done, f32[4,2]{1,0:T(4,128)S(1)} %copy.8.rate, bf16[768,144]{1,0:T(8,128)(2,1)S(1)} %get-tuple-element.6.x_table, ...), custom_call_target="tpu_custom_call" | custom-call | tf_op jit(solution)/shard_map/synthesise/pallas_call | solution.py:230
  (5 shorter events, 0.1 us)
Async XLA Ops:
  0.6 29.8 %copy-start.1 = (f32[4,2]{0,1:T(2,128)S(1)}, f32[4,2]{0,1:T(2,128)}, u32[]{:S(2)}) copy-start(f32[4,2]{0,1:T(2,128)} %param.8) | copy-start | bytes 100
  0.6 32.3 %copy-start = (f32[4,2,48,48]{3,2,1,0:T(8,128)S(1)}, f32[4,2,48,48]{3,2,1,0:T(8,128)}, u32[]{:S(2)}) copy-start(f32[4,2,48,48]{3,2,1,0:T(8,128)} %parent.1) | copy-start | bytes 221188
  3.4 4.2 %collective-permute-start = (bf16[48,384]{1,0:T(8,128)(2,1)S(1)}, bf16[48,384]{1,0:T(8,128)(2,1)S(1)}, u32[]{:S(2)}, u32[]{:S(2)}) collective-permute-start(bf16[48,384]{1,0:T(8,128)(2,1)S(1)} %get-tuple-element.5), channel_id=1, source_target_pairs={{0,32},{32,0},{4,36},{36,4},{8,40},{40,8},{12,44},{44,12},{16,48},... | collective-permute-start | bytes 110600 | tf_op jit(solution)/shard_map/total/ppermute | solution.py:81
  7.6 6.8 %collective-permute-start.4 = (bf16[48,384]{1,0:T(8,128)(2,1)S(1)}, bf16[48,384]{1,0:T(8,128)(2,1)S(1)}, u32[]{:S(2)}, u32[]{:S(2)}) collective-permute-start(bf16[48,384]{1,0:T(8,128)(2,1)S(1)} %add_convert_fusion.3), channel_id=1, source_target_pairs={{0,227},{32,0},{4,231},{36,4},{8,235},{40,8},{12,239},{44,12},{16,... | collective-permute-start | bytes 110600 | tf_op jit(solution)/shard_map/total/ppermute | solution.py:85
  8.0 6.4 %collective-permute-start.3 = (bf16[48,384]{1,0:T(8,128)(2,1)S(1)}, bf16[48,384]{1,0:T(8,128)(2,1)S(1)}, u32[]{:S(2)}, u32[]{:S(2)}) collective-permute-start(bf16[48,384]{1,0:T(8,128)(2,1)S(1)} %add_convert_fusion.3), channel_id=1, source_target_pairs={{0,35},{32,0},{4,39},{36,4},{8,43},{40,8},{12,47},{44,12},{16,51},... | collective-permute-start | bytes 110600 | tf_op jit(solution)/shard_map/total/ppermute | solution.py:85
  11.3 4.6 %collective-permute-start.2 = (bf16[48,384]{1,0:T(8,128)(2,1)S(1)}, bf16[48,384]{1,0:T(8,128)(2,1)S(1)}, u32[]{:S(2)}, u32[]{:S(2)}) collective-permute-start(bf16[48,384]{1,0:T(8,128)(2,1)S(1)} %add_convert_fusion.3), channel_id=1, source_target_pairs={{0,224},{32,0},{4,228},{36,4},{8,232},{40,8},{12,236},{44,12},{16,... | collective-permute-start | bytes 110600 | tf_op jit(solution)/shard_map/total/ppermute | solution.py:85
  11.3 4.6 %collective-permute-start.1 = (bf16[48,384]{1,0:T(8,128)(2,1)S(1)}, bf16[48,384]{1,0:T(8,128)(2,1)S(1)}, u32[]{:S(2)}, u32[]{:S(2)}) collective-permute-start(bf16[48,384]{1,0:T(8,128)(2,1)S(1)} %add_convert_fusion.3), channel_id=1, source_target_pairs={{0,32},{32,0},{4,36},{36,4},{8,40},{40,8},{12,44},{44,12},{16,48},... | collective-permute-start | bytes 110600 | tf_op jit(solution)/shard_map/total/ppermute | solution.py:88
  15.9 6.6 %collective-permute-start.8 = (bf16[48,384]{1,0:T(8,128)(2,1)S(1)}, bf16[48,384]{1,0:T(8,128)(2,1)S(1)}, u32[]{:S(2)}, u32[]{:S(2)}) collective-permute-start(bf16[48,384]{1,0:T(8,128)(2,1)S(1)} %add_convert_fusion.2), channel_id=1, source_target_pairs={{32,20},{0,32},{36,16},{4,36},{40,28},{8,40},{44,24},{12,44},{48,4... | collective-permute-start | bytes 110600 | tf_op jit(solution)/shard_map/total/ppermute | solution.py:85
  20.0 3.0 %collective-permute-start.7 = (bf16[48,384]{1,0:T(8,128)(2,1)S(1)}, bf16[48,384]{1,0:T(8,128)(2,1)S(1)}, u32[]{:S(2)}, u32[]{:S(2)}) collective-permute-start(bf16[48,384]{1,0:T(8,128)(2,1)S(1)} %add_convert_fusion.2), channel_id=1, source_target_pairs={{32,28},{0,32},{36,24},{4,36},{40,20},{8,40},{44,16},{12,44},{48,1... | collective-permute-start | bytes 110600 | tf_op jit(solution)/shard_map/total/ppermute | solution.py:85
  22.0 1.3 %collective-permute-start.6 = (bf16[48,384]{1,0:T(8,128)(2,1)S(1)}, bf16[48,384]{1,0:T(8,128)(2,1)S(1)}, u32[]{:S(2)}, u32[]{:S(2)}) collective-permute-start(bf16[48,384]{1,0:T(8,128)(2,1)S(1)} %add_convert_fusion.2), channel_id=1, source_target_pairs={{32,8},{0,32},{36,12},{4,36},{40,0},{8,40},{44,4},{12,44},{48,24},... | collective-permute-start | bytes 110600 | tf_op jit(solution)/shard_map/total/ppermute | solution.py:85
  22.0 1.4 %collective-permute-start.5 = (bf16[48,384]{1,0:T(8,128)(2,1)S(1)}, bf16[48,384]{1,0:T(8,128)(2,1)S(1)}, u32[]{:S(2)}, u32[]{:S(2)}) collective-permute-start(bf16[48,384]{1,0:T(8,128)(2,1)S(1)} %add_convert_fusion.2), channel_id=1, source_target_pairs={{0,32},{32,0},{4,36},{36,4},{8,40},{40,8},{12,44},{44,12},{16,48},... | collective-permute-start | bytes 110600 | tf_op jit(solution)/shard_map/total/ppermute | solution.py:88
  23.4 4.4 %collective-permute-start.12 = (bf16[48,384]{1,0:T(8,128)(2,1)S(1)}, bf16[48,384]{1,0:T(8,128)(2,1)S(1)}, u32[]{:S(2)}, u32[]{:S(2)}) collective-permute-start(bf16[48,384]{1,0:T(8,128)(2,1)S(1)} %add_convert_fusion.1), channel_id=1, source_target_pairs={{0,37},{32,0},{4,33},{36,4},{8,45},{40,8},{12,41},{44,12},{16,53},... | collective-permute-start | bytes 110600 | tf_op jit(solution)/shard_map/total/ppermute | solution.py:85
  26.4 3.4 %collective-permute-start.11 = (bf16[48,384]{1,0:T(8,128)(2,1)S(1)}, bf16[48,384]{1,0:T(8,128)(2,1)S(1)}, u32[]{:S(2)}, u32[]{:S(2)}) collective-permute-start(bf16[48,384]{1,0:T(8,128)(2,1)S(1)} %add_convert_fusion.1), channel_id=1, source_target_pairs={{0,36},{32,0},{4,32},{36,4},{8,44},{40,8},{12,40},{44,12},{16,52},... | collective-permute-start | bytes 110600 | tf_op jit(solution)/shard_map/total/ppermute | solution.py:85
  26.5 3.4 %collective-permute-start.10 = (bf16[48,384]{1,0:T(8,128)(2,1)S(1)}, bf16[48,384]{1,0:T(8,128)(2,1)S(1)}, u32[]{:S(2)}, u32[]{:S(2)}) collective-permute-start(bf16[48,384]{1,0:T(8,128)(2,1)S(1)} %add_convert_fusion.1), channel_id=1, source_target_pairs={{0,33},{32,0},{4,37},{36,4},{8,41},{40,8},{12,45},{44,12},{16,49},... | collective-permute-start | bytes 110600 | tf_op jit(solution)/shard_map/total/ppermute | solution.py:85
  26.8 3.0 %collective-permute-start.9 = (bf16[48,384]{1,0:T(8,128)(2,1)S(1)}, bf16[48,384]{1,0:T(8,128)(2,1)S(1)}, u32[]{:S(2)}, u32[]{:S(2)}) collective-permute-start(bf16[48,384]{1,0:T(8,128)(2,1)S(1)} %add_convert_fusion.1), channel_id=1, source_target_pairs={{0,32},{32,0},{4,36},{36,4},{8,40},{40,8},{12,44},{44,12},{16,48},... | collective-permute-start | bytes 110600 | tf_op jit(solution)/shard_map/total/ppermute | solution.py:88
  29.9 1.3 %collective-permute-start.15 = (bf16[48,384]{1,0:T(8,128)(2,1)S(1)}, bf16[48,384]{1,0:T(8,128)(2,1)S(1)}, u32[]{:S(2)}, u32[]{:S(2)}) collective-permute-start(bf16[48,384]{1,0:T(8,128)(2,1)S(1)} %add_convert_fusion), channel_id=1, source_target_pairs={{32,64},{0,32},{36,68},{4,36},{40,72},{8,40},{44,76},{12,44},{48,8... | collective-permute-start | bytes 110600 | tf_op jit(solution)/shard_map/total/ppermute | solution.py:92
  30.0 2.9 %collective-permute-start.14 = (bf16[48,384]{1,0:T(8,128)(2,1)S(1)}, bf16[48,384]{1,0:T(8,128)(2,1)S(1)}, u32[]{:S(2)}, u32[]{:S(2)}) collective-permute-start(bf16[48,384]{1,0:T(8,128)(2,1)S(1)} %add_convert_fusion), channel_id=1, source_target_pairs={{0,64},{32,96},{4,68},{36,100},{8,72},{40,104},{12,76},{44,108},{1... | collective-permute-start | bytes 110600 | tf_op jit(solution)/shard_map/total/ppermute | solution.py:93
  30.1 2.7 %collective-permute-start.13 = (bf16[48,384]{1,0:T(8,128)(2,1)S(1)}, bf16[48,384]{1,0:T(8,128)(2,1)S(1)}, u32[]{:S(2)}, u32[]{:S(2)}) collective-permute-start(bf16[48,384]{1,0:T(8,128)(2,1)S(1)} %add_convert_fusion), channel_id=1, source_target_pairs={{0,32},{32,0},{4,36},{36,4},{8,40},{40,8},{12,44},{44,12},{16,48},... | collective-permute-start | bytes 110600 | tf_op jit(solution)/shard_map/total/ppermute | solution.py:94

commit v3 on v2

--- a/solution.py
+++ b/solution.py
@@ -13,8 +13,8 @@
 KW = 24
 MODES = 2 * KW
 FLAT = 8
-PIECE = 16
-WIDTH = 3 * FLAT * PIECE
+WIDTH = FLAT * MODES
+SPECTRA_AFTER = 3
 AXES = ("x", "c", "z", "y")
 SIZES = {"x": 4, "c": 2, "z": 8, "y": 4}
 CHIPS = [(x, y, z) for x in range(4) for y in range(4) for z in range(8)]
@@ -64,8 +64,8 @@
 FLIP_Z0 = lambda x, y, z: (x, y, z ^ 1)
 FLIP_Z1 = lambda x, y, z: (x, y, z ^ 2)
 FLIP_Z2 = lambda x, y, z: (x, y, 7 - z)
-STAGES = ((FLIP_X1, FLIP_Y1), (FLIP_Z1, FLIP_Z2), (FLIP_Y0, FLIP_Z0))
-LAST = FLIP_X0
+STAGES = ((FLIP_X0, FLIP_Y0), (FLIP_Z0, FLIP_Z1), (FLIP_X1, FLIP_Y1))
+LAST = FLIP_Z2
 
 
 def on_both(move):
@@ -99,7 +99,7 @@
 
 def mask_of(flat, rows):
     lane = lax.broadcasted_iota(jnp.int32, (rows, WIDTH), 1)
-    return lane // PIECE % FLAT == flat
+    return (lane >= flat * MODES) & (lane < (flat + 1) * MODES)
 
 
 def dot(a, b, dims=((1,), (0,))):
@@ -135,11 +135,8 @@
         copy.start()
     copy_wide.start()
     copy_y.wait()
-    row = lax.broadcasted_iota(jnp.int32, (WIDTH, MODES), 0)
-    mode = lax.broadcasted_iota(jnp.int32, (WIDTH, MODES), 1)
-    spread = (row // 128 * PIECE + row % PIECE == mode).astype(jnp.bfloat16)
-    y_high = dot(spread, y_table[:MODES]).astype(jnp.bfloat16)
-    y_low = dot(spread, y_table[MODES:]).astype(jnp.bfloat16)
+    y_high = jnp.concatenate([y_table[:MODES]] * FLAT)
+    y_low = jnp.concatenate([y_table[MODES:]] * FLAT)
     copy_x.wait()
     for pair in range(0, FLAT, 2):
         copies[pair].wait()
@@ -158,32 +155,34 @@
     copy_wide.wait()
 
 
-def synthesise(sums, parent, rate, x_table, y_table, out, spectra, blocks, sems):
+def synthesise(sums, parent, rate, x_table, y_table, out, spectra, blocks, modes, sems):
+    y_high, y_low = y_table[:MODES], y_table[MODES:]
+    p_high, p_low = split(jnp.concatenate([parent[f // 2, f % 2] for f in range(FLAT)]))
+    wanted = dot(p_high, y_high) + dot(p_low, y_high) + dot(p_high, y_low)
     high, low = split(sums[...])
     none = jnp.zeros((MODES, WIDTH), jnp.bfloat16)
     highs = jnp.concatenate([jnp.where(mask_of(f, MODES), high, none) for f in range(FLAT)])
     lows = jnp.concatenate([jnp.where(mask_of(f, MODES), low, none) for f in range(FLAT)])
+    y_high, y_low = jnp.concatenate([y_high] * FLAT), jnp.concatenate([y_low] * FLAT)
+    found = dot(highs, y_high) + dot(lows, y_high) + dot(highs, y_low)
     row = lax.broadcasted_iota(jnp.int32, (WIDTH, MODES), 0)
     mode = lax.broadcasted_iota(jnp.int32, (WIDTH, MODES), 1)
-    gather = (row // 128 * PIECE + row % PIECE == mode).astype(jnp.bfloat16)
-    coeffs = dot(highs, gather) + dot(lows, gather)
-    y_high, y_low = y_table[:MODES], y_table[MODES:]
-    rows = []
-    for f in range(FLAT):
-        mine = coeffs[f * MODES : (f + 1) * MODES]
-        spectra[f // 2, f % 2] = mine
-        rows.append((rate[f // 2, f % 2] / MODES) * (parent[f // 2, f % 2] - mine))
-    d_high, d_low = split(jnp.concatenate(rows))
-    across = dot(d_high, y_high) + dot(d_low, y_high) + dot(d_high, y_low)
-    a_high, a_low = split(across)
+    gather = (row % MODES == mode).astype(jnp.bfloat16)
     copies = []
     for f in range(FLAT):
         mine = slice(f * MODES, (f + 1) * MODES)
-        weights = jnp.concatenate([a_high[mine], a_high[mine], a_low[mine]])
+        pull = rate[f // 2 : f // 2 + 1, f % 2 : f % 2 + 1] / MODES
+        a_high, a_low = split(pull * (wanted[mine] - found[mine]))
+        weights = jnp.concatenate([a_high, a_high, a_low])
         blocks[f] = dot(x_table[...], weights).astype(jnp.bfloat16)
-        copy = pltpu.make_async_copy(blocks.at[f], out.at[f // 2, f % 2], sems.at[f])
-        copy.start()
-        copies.append(copy)
+        copies.append(pltpu.make_async_copy(blocks.at[f], out.at[f // 2, f % 2], sems.at[f]))
+        copies[-1].start()
+        if f == SPECTRA_AFTER:
+            coeffs = dot(highs, gather) + dot(lows, gather)
+            for g in range(FLAT):
+                modes[g // 2, g % 2] = coeffs[g * MODES : (g + 1) * MODES]
+            copies.append(pltpu.make_async_copy(modes, spectra, sems.at[FLAT]))
+            copies[-1].start()
     for copy in copies:
         copy.wait()
 
@@ -233,11 +232,12 @@
                 jax.ShapeDtypeStruct((4, 2, cols_x, cols_y), jnp.bfloat16),
                 jax.ShapeDtypeStruct((4, 2, MODES, MODES), jnp.float32),
             ),
-            in_specs=[vmem, vmem, pl.BlockSpec(memory_space=pltpu.SMEM), vmem, vmem],
-            out_specs=(any_space, vmem),
+            in_specs=[vmem] * 5,
+            out_specs=(any_space, any_space),
             scratch_shapes=[
                 pltpu.VMEM((FLAT, cols_x, cols_y), jnp.bfloat16),
-                pltpu.SemaphoreType.DMA((FLAT,)),
+                pltpu.VMEM((4, 2, MODES, MODES), jnp.float32),
+                pltpu.SemaphoreType.DMA((FLAT + 1,)),
             ],
             compiler_params=pltpu.CompilerParams(vmem_limit_bytes=16 << 20),
             name="synthesise",

time: 37 us -> 35.5 us (0.959)
  Pallas kernels: 6.72 us -> 5.71 us
  starting transfers between devices: 18.4 us -> 17.9 us
    ppermute x9, starting transfers between devices: 13.2 us -> 8.97 us  [total_of(): lax.ppermute(value, AXES, hand_over(core, move)).astype(jnp.float32)]
    ppermute x1, starting transfers between devices: 0.16 us -> 1.91 us  [total_of(): straight = lax.ppermute(value, AXES, on_both(LAST))]
    ppermute x1, starting transfers between devices: 0.08 us -> 1.26 us  [total_of(): crossed = lax.ppermute(value, AXES, hand_over(core, LAST))]
    pallas_call x1, Pallas kernels: 3.96 us -> 3 us  [per_device(): pl.pallas_call(synthesise, out_shape=(jax.ShapeDtypeStruct((4, 2, cols_x,...]
    ppermute x1, waiting for transfers between devices: 0.6 us -> 0.01 us  [total_of(): crossed = lax.ppermute(value, AXES, hand_over(core, LAST))]
    ppermute x3, starting transfers between devices: 1.29 us -> 1.77 us  [total_of(): own = lax.ppermute(value, AXES, swap_cores()).astype(jnp.float32)]
  transfers between devices with their start and end apart: 16 -> 16, of which waited for: 11 -> 8; matrix products, arithmetic and copies ran while one was open for 0% -> 0% of each run, Pallas kernels for 0% -> 0%
where the time goes in v3:
time: 35.5 us; the launch traced here: 35.2 us
  starting transfers between devices  17.9 us (50%)
  waiting for transfers between devices  10.7 us (30%)
  Pallas kernels  5.71 us (16%)
  between operations  0.7 us (2%)
    ppermute x9, starting transfers between devices, total_of(): lax.ppermute(value, AXES, hand_over(core, move)).astype(jnp.float32)  8.97 us
    ppermute x9, waiting for transfers between devices, total_of(): lax.ppermute(value, AXES, hand_over(core, move)).astype(jnp.float32)  7.72 us
    ppermute x1, starting transfers between devices, total_of(): lax.ppermute(half, AXES, swap_cores()).astype(jnp.float32)  3.33 us
    pallas_call x1, Pallas kernels, per_device(): pl.pallas_call(synthesise, out_shape=(jax.ShapeDtypeStruct((4, 2, cols_x,...  3 us
    pallas_call x1, Pallas kernels, per_device(): pl.pallas_call(lambda *refs: analyse(scale, *refs), out_shape=(small, jax...  2.7 us
    ppermute x1, waiting for transfers between devices, total_of(): straight = lax.ppermute(value, AXES, on_both(LAST))  2.06 us
    ppermute x1, starting transfers between devices, total_of(): straight = lax.ppermute(value, AXES, on_both(LAST))  1.91 us
    ppermute x3, starting transfers between devices, total_of(): own = lax.ppermute(value, AXES, swap_cores()).astype(jnp.float32)  1.77 us
  transfers between devices with their start and end apart: 16, of which 8 were waited for; matrix products, arithmetic and copies ran while one was open for 0% of the time, Pallas kernels for 0%

profile of v3, /device:TPU:1, one launch (start us, length us, event | category | flops | bytes accessed | tf_op | source)
XLA Modules:
  0.0 35.2 jit_solution(11719439922962325547)
XLA Ops:
  0.6 0.0 copy-start.1
  0.6 0.0 copy-start
  0.6 2.7 %analyse.1 = (bf16[48,384]{1,0:T(8,128)(2,1)S(1)}, bf16[768,144]{1,0:T(8,128)(2,1)S(1)}, bf16[96,256]{1,0:T(8,128)(2,1)S(1)}) custom-call(bf16[4,2,768,256]{3,2,1,0:T(8,128)(2,1)} %refs_0_.1, bf16[8,256,768]{2,1,0:T(8,128)(2,1)} %constant.14.clone.refs_1_, bf16[32,192,256]{2,1,0:T(8,128)(2,1)} %constant.15.clone.refs_2_, ...), custom_call_target="tpu_custom_call" | custom-call | tf_op jit(solution)/shard_map/analyse/pallas_call | solution.py:208
  3.4 3.3 %collective-permute-start = (bf16[48,384]{1,0:T(8,128)(2,1)S(1)}, bf16[48,384]{1,0:T(8,128)(2,1)S(1)}, u32[]{:S(2)}, u32[]{:S(2)}) collective-permute-start(bf16[48,384]{1,0:T(8,128)(2,1)S(1)} %get-tuple-element.5), channel_id=1, source_target_pairs={{0,32},{32,0},{4,36},{36,4},{8,40},{40,8},{12,44},{44,12},{16,48},... | collective-permute-start | bytes 110600 | tf_op jit(solution)/shard_map/total/ppermute | solution.py:81
  6.7 0.9 %collective-permute-done = bf16[48,384]{1,0:T(8,128)(2,1)S(1)} collective-permute-done((bf16[48,384]{1,0:T(8,128)(2,1)S(1)}, bf16[48,384]{1,0:T(8,128)(2,1)S(1)}, u32[]{:S(2)}, u32[]{:S(2)}) %collective-permute-start) | collective-permute-done | bytes 36896 | tf_op jit(solution)/shard_map/total/ppermute | solution.py:81
  7.6 0.4 %collective-permute-start.4 = (bf16[48,384]{1,0:T(8,128)(2,1)S(1)}, bf16[48,384]{1,0:T(8,128)(2,1)S(1)}, u32[]{:S(2)}, u32[]{:S(2)}) collective-permute-start(bf16[48,384]{1,0:T(8,128)(2,1)S(1)} %add_convert_fusion.3), channel_id=1, source_target_pairs={{0,97},{32,0},{4,101},{36,4},{8,105},{40,8},{12,109},{44,12},{16,1... | collective-permute-start | bytes 110600 | tf_op jit(solution)/shard_map/total/ppermute | solution.py:85
  8.0 0.5 %collective-permute-start.3 = (bf16[48,384]{1,0:T(8,128)(2,1)S(1)}, bf16[48,384]{1,0:T(8,128)(2,1)S(1)}, u32[]{:S(2)}, u32[]{:S(2)}) collective-permute-start(bf16[48,384]{1,0:T(8,128)(2,1)S(1)} %add_convert_fusion.3), channel_id=1, source_target_pairs={{0,33},{32,0},{4,37},{36,4},{8,41},{40,8},{12,45},{44,12},{16,49},... | collective-permute-start | bytes 110600 | tf_op jit(solution)/shard_map/total/ppermute | solution.py:85
  8.5 0.0 collective-permute-start.2
  8.5 0.6 %collective-permute-start.1 = (bf16[48,384]{1,0:T(8,128)(2,1)S(1)}, bf16[48,384]{1,0:T(8,128)(2,1)S(1)}, u32[]{:S(2)}, u32[]{:S(2)}) collective-permute-start(bf16[48,384]{1,0:T(8,128)(2,1)S(1)} %add_convert_fusion.3), channel_id=1, source_target_pairs={{0,32},{32,0},{4,36},{36,4},{8,40},{40,8},{12,44},{44,12},{16,48},... | collective-permute-start | bytes 110600 | tf_op jit(solution)/shard_map/total/ppermute | solution.py:88
  9.2 2.7 %collective-permute-done.4 = bf16[48,384]{1,0:T(8,128)(2,1)S(1)} collective-permute-done((bf16[48,384]{1,0:T(8,128)(2,1)S(1)}, bf16[48,384]{1,0:T(8,128)(2,1)S(1)}, u32[]{:S(2)}, u32[]{:S(2)}) %collective-permute-start.4) | collective-permute-done | bytes 36896 | tf_op jit(solution)/shard_map/total/ppermute | solution.py:85
  11.9 0.0 collective-permute-done.3
  11.9 0.0 collective-permute-done.2
  11.9 0.0 collective-permute-done.1
  12.0 3.2 %collective-permute-start.8 = (bf16[48,384]{1,0:T(8,128)(2,1)S(1)}, bf16[48,384]{1,0:T(8,128)(2,1)S(1)}, u32[]{:S(2)}, u32[]{:S(2)}) collective-permute-start(bf16[48,384]{1,0:T(8,128)(2,1)S(1)} %add_convert_fusion.2), channel_id=1, source_target_pairs={{32,12},{0,32},{36,8},{4,36},{40,4},{8,40},{44,0},{12,44},{48,28},... | collective-permute-start | bytes 110600 | tf_op jit(solution)/shard_map/total/ppermute | solution.py:85
  15.2 0.3 collective-permute-start.7
  15.4 0.0 collective-permute-start.6
  15.4 0.5 %collective-permute-start.5 = (bf16[48,384]{1,0:T(8,128)(2,1)S(1)}, bf16[48,384]{1,0:T(8,128)(2,1)S(1)}, u32[]{:S(2)}, u32[]{:S(2)}) collective-permute-start(bf16[48,384]{1,0:T(8,128)(2,1)S(1)} %add_convert_fusion.2), channel_id=1, source_target_pairs={{0,32},{32,0},{4,36},{36,4},{8,40},{40,8},{12,44},{44,12},{16,48},... | collective-permute-start | bytes 110600 | tf_op jit(solution)/shard_map/total/ppermute | solution.py:88
  15.9 0.3 collective-permute-done.8
  16.2 0.3 collective-permute-done.7
  16.6 0.3 collective-permute-done.6
  16.9 0.0 collective-permute-done.5
  16.9 2.2 %collective-permute-start.12 = (bf16[48,384]{1,0:T(8,128)(2,1)S(1)}, bf16[48,384]{1,0:T(8,128)(2,1)S(1)}, u32[]{:S(2)}, u32[]{:S(2)}) collective-permute-start(bf16[48,384]{1,0:T(8,128)(2,1)S(1)} %add_convert_fusion.1), channel_id=1, source_target_pairs={{0,227},{32,0},{4,231},{36,4},{8,235},{40,8},{12,239},{44,12},{16,... | collective-permute-start | bytes 110600 | tf_op jit(solution)/shard_map/total/ppermute | solution.py:85
  19.2 2.3 %collective-permute-start.11 = (bf16[48,384]{1,0:T(8,128)(2,1)S(1)}, bf16[48,384]{1,0:T(8,128)(2,1)S(1)}, u32[]{:S(2)}, u32[]{:S(2)}) collective-permute-start(bf16[48,384]{1,0:T(8,128)(2,1)S(1)} %add_convert_fusion.1), channel_id=1, source_target_pairs={{0,35},{32,0},{4,39},{36,4},{8,43},{40,8},{12,47},{44,12},{16,51},... | collective-permute-start | bytes 110600 | tf_op jit(solution)/shard_map/total/ppermute | solution.py:85
  21.5 0.0 collective-permute-start.10
  21.5 0.6 %collective-permute-start.9 = (bf16[48,384]{1,0:T(8,128)(2,1)S(1)}, bf16[48,384]{1,0:T(8,128)(2,1)S(1)}, u32[]{:S(2)}, u32[]{:S(2)}) collective-permute-start(bf16[48,384]{1,0:T(8,128)(2,1)S(1)} %add_convert_fusion.1), channel_id=1, source_target_pairs={{0,32},{32,0},{4,36},{36,4},{8,40},{40,8},{12,44},{44,12},{16,48},... | collective-permute-start | bytes 110600 | tf_op jit(solution)/shard_map/total/ppermute | solution.py:88
  22.1 2.7 %collective-permute-done.12 = bf16[48,384]{1,0:T(8,128)(2,1)S(1)} collective-permute-done((bf16[48,384]{1,0:T(8,128)(2,1)S(1)}, bf16[48,384]{1,0:T(8,128)(2,1)S(1)}, u32[]{:S(2)}, u32[]{:S(2)}) %collective-permute-start.12) | collective-permute-done | bytes 36896 | tf_op jit(solution)/shard_map/total/ppermute | solution.py:85
  24.8 0.0 collective-permute-done.11
  24.8 1.3 %collective-permute-done.10 = bf16[48,384]{1,0:T(8,128)(2,1)S(1)} collective-permute-done((bf16[48,384]{1,0:T(8,128)(2,1)S(1)}, bf16[48,384]{1,0:T(8,128)(2,1)S(1)}, u32[]{:S(2)}, u32[]{:S(2)}) %collective-permute-start.10) | collective-permute-done | bytes 36896 | tf_op jit(solution)/shard_map/total/ppermute | solution.py:85
  26.1 0.0 collective-permute-done.9
  26.1 1.3 %collective-permute-start.15 = (bf16[48,384]{1,0:T(8,128)(2,1)S(1)}, bf16[48,384]{1,0:T(8,128)(2,1)S(1)}, u32[]{:S(2)}, u32[]{:S(2)}) collective-permute-start(bf16[48,384]{1,0:T(8,128)(2,1)S(1)} %add_convert_fusion), channel_id=1, source_target_pairs={{32,28},{0,32},{36,24},{4,36},{40,20},{8,40},{44,16},{12,44},{48,1... | collective-permute-start | bytes 110600 | tf_op jit(solution)/shard_map/total/ppermute | solution.py:92
  27.4 1.9 %collective-permute-start.14 = (bf16[48,384]{1,0:T(8,128)(2,1)S(1)}, bf16[48,384]{1,0:T(8,128)(2,1)S(1)}, u32[]{:S(2)}, u32[]{:S(2)}) collective-permute-start(bf16[48,384]{1,0:T(8,128)(2,1)S(1)} %add_convert_fusion), channel_id=1, source_target_pairs={{0,28},{32,60},{4,24},{36,56},{8,20},{40,52},{12,16},{44,48},{16,1... | collective-permute-start | bytes 110600 | tf_op jit(solution)/shard_map/total/ppermute | solution.py:93
  29.3 0.7 %collective-permute-start.13 = (bf16[48,384]{1,0:T(8,128)(2,1)S(1)}, bf16[48,384]{1,0:T(8,128)(2,1)S(1)}, u32[]{:S(2)}, u32[]{:S(2)}) collective-permute-start(bf16[48,384]{1,0:T(8,128)(2,1)S(1)} %add_convert_fusion), channel_id=1, source_target_pairs={{0,32},{32,0},{4,36},{36,4},{8,40},{40,8},{12,44},{44,12},{16,48},... | collective-permute-start | bytes 110600 | tf_op jit(solution)/shard_map/total/ppermute | solution.py:94
  30.0 0.0 copy-done.1
  30.0 0.1 copy.8.rate
  30.1 0.0 collective-permute-done.15
  30.1 2.1 %collective-permute-done.14 = bf16[48,384]{1,0:T(8,128)(2,1)S(1)} collective-permute-done((bf16[48,384]{1,0:T(8,128)(2,1)S(1)}, bf16[48,384]{1,0:T(8,128)(2,1)S(1)}, u32[]{:S(2)}, u32[]{:S(2)}) %collective-permute-start.14) | collective-permute-done | bytes 36896 | tf_op jit(solution)/shard_map/total/ppermute | solution.py:93
  32.2 0.0 collective-permute-done.13
  32.2 0.0 copy-done
  32.2 3.0 %synthesise.1 = (bf16[4,2,768,256]{3,2,1,0:T(8,128)(2,1)}, f32[4,2,48,48]{3,2,1,0:T(8,128)}) custom-call(f32[48,384]{1,0:T(8,128)S(1)} %convert_add_fusion.sums, f32[4,2,48,48]{3,2,1,0:T(8,128)S(1)} %copy-done, f32[4,2]{1,0:T(4,128)S(1)} %copy.8.rate, bf16[768,144]{1,0:T(8,128)(2,1)S(1)} %get-tuple-element.6.x_table, ...), custom_call_target="tpu_custom_call" | custom-call | tf_op jit(solution)/shard_map/synthesise/pallas_call | solution.py:229
  (5 shorter events, 0.1 us)
Async XLA Ops:
  0.6 29.4 %copy-start.1 = (f32[4,2]{0,1:T(2,128)S(1)}, f32[4,2]{0,1:T(2,128)}, u32[]{:S(2)}) copy-start(f32[4,2]{0,1:T(2,128)} %param.8) | copy-start | bytes 100
  0.6 31.6 %copy-start = (f32[4,2,48,48]{3,2,1,0:T(8,128)S(1)}, f32[4,2,48,48]{3,2,1,0:T(8,128)}, u32[]{:S(2)}) copy-start(f32[4,2,48,48]{3,2,1,0:T(8,128)} %parent.1) | copy-start | bytes 221188
  3.4 4.2 %collective-permute-start = (bf16[48,384]{1,0:T(8,128)(2,1)S(1)}, bf16[48,384]{1,0:T(8,128)(2,1)S(1)}, u32[]{:S(2)}, u32[]{:S(2)}) collective-permute-start(bf16[48,384]{1,0:T(8,128)(2,1)S(1)} %get-tuple-element.5), channel_id=1, source_target_pairs={{0,32},{32,0},{4,36},{36,4},{8,40},{40,8},{12,44},{44,12},{16,48},... | collective-permute-start | bytes 110600 | tf_op jit(solution)/shard_map/total/ppermute | solution.py:81
  7.6 4.4 %collective-permute-start.4 = (bf16[48,384]{1,0:T(8,128)(2,1)S(1)}, bf16[48,384]{1,0:T(8,128)(2,1)S(1)}, u32[]{:S(2)}, u32[]{:S(2)}) collective-permute-start(bf16[48,384]{1,0:T(8,128)(2,1)S(1)} %add_convert_fusion.3), channel_id=1, source_target_pairs={{0,97},{32,0},{4,101},{36,4},{8,105},{40,8},{12,109},{44,12},{16,1... | collective-permute-start | bytes 110600 | tf_op jit(solution)/shard_map/total/ppermute | solution.py:85
  8.0 3.9 %collective-permute-start.3 = (bf16[48,384]{1,0:T(8,128)(2,1)S(1)}, bf16[48,384]{1,0:T(8,128)(2,1)S(1)}, u32[]{:S(2)}, u32[]{:S(2)}) collective-permute-start(bf16[48,384]{1,0:T(8,128)(2,1)S(1)} %add_convert_fusion.3), channel_id=1, source_target_pairs={{0,33},{32,0},{4,37},{36,4},{8,41},{40,8},{12,45},{44,12},{16,49},... | collective-permute-start | bytes 110600 | tf_op jit(solution)/shard_map/total/ppermute | solution.py:85
  8.5 3.4 %collective-permute-start.2 = (bf16[48,384]{1,0:T(8,128)(2,1)S(1)}, bf16[48,384]{1,0:T(8,128)(2,1)S(1)}, u32[]{:S(2)}, u32[]{:S(2)}) collective-permute-start(bf16[48,384]{1,0:T(8,128)(2,1)S(1)} %add_convert_fusion.3), channel_id=1, source_target_pairs={{0,96},{32,0},{4,100},{36,4},{8,104},{40,8},{12,108},{44,12},{16,1... | collective-permute-start | bytes 110600 | tf_op jit(solution)/shard_map/total/ppermute | solution.py:85
  8.5 3.4 %collective-permute-start.1 = (bf16[48,384]{1,0:T(8,128)(2,1)S(1)}, bf16[48,384]{1,0:T(8,128)(2,1)S(1)}, u32[]{:S(2)}, u32[]{:S(2)}) collective-permute-start(bf16[48,384]{1,0:T(8,128)(2,1)S(1)} %add_convert_fusion.3), channel_id=1, source_target_pairs={{0,32},{32,0},{4,36},{36,4},{8,40},{40,8},{12,44},{44,12},{16,48},... | collective-permute-start | bytes 110600 | tf_op jit(solution)/shard_map/total/ppermute | solution.py:88
  12.0 4.2 %collective-permute-start.8 = (bf16[48,384]{1,0:T(8,128)(2,1)S(1)}, bf16[48,384]{1,0:T(8,128)(2,1)S(1)}, u32[]{:S(2)}, u32[]{:S(2)}) collective-permute-start(bf16[48,384]{1,0:T(8,128)(2,1)S(1)} %add_convert_fusion.2), channel_id=1, source_target_pairs={{32,12},{0,32},{36,8},{4,36},{40,4},{8,40},{44,0},{12,44},{48,28},... | collective-permute-start | bytes 110600 | tf_op jit(solution)/shard_map/total/ppermute | solution.py:85
  15.2 1.4 %collective-permute-start.7 = (bf16[48,384]{1,0:T(8,128)(2,1)S(1)}, bf16[48,384]{1,0:T(8,128)(2,1)S(1)}, u32[]{:S(2)}, u32[]{:S(2)}) collective-permute-start(bf16[48,384]{1,0:T(8,128)(2,1)S(1)} %add_convert_fusion.2), channel_id=1, source_target_pairs={{32,8},{0,32},{36,12},{4,36},{40,0},{8,40},{44,4},{12,44},{48,24},... | collective-permute-start | bytes 110600 | tf_op jit(solution)/shard_map/total/ppermute | solution.py:85
  15.4 1.5 %collective-permute-start.6 = (bf16[48,384]{1,0:T(8,128)(2,1)S(1)}, bf16[48,384]{1,0:T(8,128)(2,1)S(1)}, u32[]{:S(2)}, u32[]{:S(2)}) collective-permute-start(bf16[48,384]{1,0:T(8,128)(2,1)S(1)} %add_convert_fusion.2), channel_id=1, source_target_pairs={{32,4},{0,32},{36,0},{4,36},{40,12},{8,40},{44,8},{12,44},{48,20},... | collective-permute-start | bytes 110600 | tf_op jit(solution)/shard_map/total/ppermute | solution.py:85
  15.4 1.5 %collective-permute-start.5 = (bf16[48,384]{1,0:T(8,128)(2,1)S(1)}, bf16[48,384]{1,0:T(8,128)(2,1)S(1)}, u32[]{:S(2)}, u32[]{:S(2)}) collective-permute-start(bf16[48,384]{1,0:T(8,128)(2,1)S(1)} %add_convert_fusion.2), channel_id=1, source_target_pairs={{0,32},{32,0},{4,36},{36,4},{8,40},{40,8},{12,44},{44,12},{16,48},... | collective-permute-start | bytes 110600 | tf_op jit(solution)/shard_map/total/ppermute | solution.py:88
  16.9 7.8 %collective-permute-start.12 = (bf16[48,384]{1,0:T(8,128)(2,1)S(1)}, bf16[48,384]{1,0:T(8,128)(2,1)S(1)}, u32[]{:S(2)}, u32[]{:S(2)}) collective-permute-start(bf16[48,384]{1,0:T(8,128)(2,1)S(1)} %add_convert_fusion.1), channel_id=1, source_target_pairs={{0,227},{32,0},{4,231},{36,4},{8,235},{40,8},{12,239},{44,12},{16,... | collective-permute-start | bytes 110600 | tf_op jit(solution)/shard_map/total/ppermute | solution.py:85
  19.2 5.6 %collective-permute-start.11 = (bf16[48,384]{1,0:T(8,128)(2,1)S(1)}, bf16[48,384]{1,0:T(8,128)(2,1)S(1)}, u32[]{:S(2)}, u32[]{:S(2)}) collective-permute-start(bf16[48,384]{1,0:T(8,128)(2,1)S(1)} %add_convert_fusion.1), channel_id=1, source_target_pairs={{0,35},{32,0},{4,39},{36,4},{8,43},{40,8},{12,47},{44,12},{16,51},... | collective-permute-start | bytes 110600 | tf_op jit(solution)/shard_map/total/ppermute | solution.py:85
  21.5 4.6 %collective-permute-start.10 = (bf16[48,384]{1,0:T(8,128)(2,1)S(1)}, bf16[48,384]{1,0:T(8,128)(2,1)S(1)}, u32[]{:S(2)}, u32[]{:S(2)}) collective-permute-start(bf16[48,384]{1,0:T(8,128)(2,1)S(1)} %add_convert_fusion.1), channel_id=1, source_target_pairs={{0,224},{32,0},{4,228},{36,4},{8,232},{40,8},{12,236},{44,12},{16,... | collective-permute-start | bytes 110600 | tf_op jit(solution)/shard_map/total/ppermute | solution.py:85
  21.5 4.6 %collective-permute-start.9 = (bf16[48,384]{1,0:T(8,128)(2,1)S(1)}, bf16[48,384]{1,0:T(8,128)(2,1)S(1)}, u32[]{:S(2)}, u32[]{:S(2)}) collective-permute-start(bf16[48,384]{1,0:T(8,128)(2,1)S(1)} %add_convert_fusion.1), channel_id=1, source_target_pairs={{0,32},{32,0},{4,36},{36,4},{8,40},{40,8},{12,44},{44,12},{16,48},... | collective-permute-start | bytes 110600 | tf_op jit(solution)/shard_map/total/ppermute | solution.py:88
  26.1 4.0 %collective-permute-start.15 = (bf16[48,384]{1,0:T(8,128)(2,1)S(1)}, bf16[48,384]{1,0:T(8,128)(2,1)S(1)}, u32[]{:S(2)}, u32[]{:S(2)}) collective-permute-start(bf16[48,384]{1,0:T(8,128)(2,1)S(1)} %add_convert_fusion), channel_id=1, source_target_pairs={{32,28},{0,32},{36,24},{4,36},{40,20},{8,40},{44,16},{12,44},{48,1... | collective-permute-start | bytes 110600 | tf_op jit(solution)/shard_map/total/ppermute | solution.py:92
  27.4 4.8 %collective-permute-start.14 = (bf16[48,384]{1,0:T(8,128)(2,1)S(1)}, bf16[48,384]{1,0:T(8,128)(2,1)S(1)}, u32[]{:S(2)}, u32[]{:S(2)}) collective-permute-start(bf16[48,384]{1,0:T(8,128)(2,1)S(1)} %add_convert_fusion), channel_id=1, source_target_pairs={{0,28},{32,60},{4,24},{36,56},{8,20},{40,52},{12,16},{44,48},{16,1... | collective-permute-start | bytes 110600 | tf_op jit(solution)/shard_map/total/ppermute | solution.py:93
  29.3 2.9 %collective-permute-start.13 = (bf16[48,384]{1,0:T(8,128)(2,1)S(1)}, bf16[48,384]{1,0:T(8,128)(2,1)S(1)}, u32[]{:S(2)}, u32[]{:S(2)}) collective-permute-start(bf16[48,384]{1,0:T(8,128)(2,1)S(1)} %add_convert_fusion), channel_id=1, source_target_pairs={{0,32},{32,0},{4,36},{36,4},{8,40},{40,8},{12,44},{44,12},{16,48},... | collective-permute-start | bytes 110600 | tf_op jit(solution)/shard_map/total/ppermute | solution.py:94

commit v4 on v3

--- a/solution.py
+++ b/solution.py
@@ -89,12 +89,11 @@
         running = (own + near[0]) + (near[1] + near[2])
         core = 1 - core
     value = running.astype(jnp.bfloat16)
-    crossed = lax.ppermute(value, AXES, hand_over(core, LAST))
-    straight = lax.ppermute(value, AXES, on_both(LAST))
-    own = lax.ppermute(value, AXES, swap_cores())
-    holds = lax.axis_index("c") == core
-    own = jnp.where(holds, value, own).astype(jnp.float32)
-    return own + jnp.where(holds, straight, crossed).astype(jnp.float32)
+    crossed = lax.ppermute(value, AXES, hand_over(core, LAST)).astype(jnp.float32)
+    own = lax.ppermute(value, AXES, swap_cores()).astype(jnp.float32)
+    total = (own + crossed).astype(jnp.bfloat16)
+    other = lax.ppermute(total, AXES, swap_cores())
+    return jnp.where(lax.axis_index("c") == core, other, total)
 
 
 def mask_of(flat, rows):
@@ -125,8 +124,8 @@
     copy_x = pltpu.make_async_copy(x_tables.at[gx, pl.ds(0, MODES)], x_table, sems.at[FLAT + 1])
     copy_wide = pltpu.make_async_copy(x_wides.at[gx], x_wide, sems.at[FLAT + 2])
     copies = [
-        pltpu.make_async_copy(fields.at[f // 2, f % 2], blocks.at[f], sems.at[f])
-        for f in range(FLAT)
+        pltpu.make_async_copy(fields.at[f], blocks.at[pl.ds(2 * f, 2)], sems.at[f])
+        for f in range(FLAT // 2)
     ]
     copies[0].start()
     copy_x.start()
@@ -139,8 +138,7 @@
     y_low = jnp.concatenate([y_table[MODES:]] * FLAT)
     copy_x.wait()
     for pair in range(0, FLAT, 2):
-        copies[pair].wait()
-        copies[pair + 1].wait()
+        copies[pair // 2].wait()
         for f in (pair, pair + 1):
             mine = pl.ds(f * MODES, MODES)
             high[mine], low[mine] = split(dot(x_table[...], blocks[f]))
@@ -159,12 +157,11 @@
     y_high, y_low = y_table[:MODES], y_table[MODES:]
     p_high, p_low = split(jnp.concatenate([parent[f // 2, f % 2] for f in range(FLAT)]))
     wanted = dot(p_high, y_high) + dot(p_low, y_high) + dot(p_high, y_low)
-    high, low = split(sums[...])
+    high = sums[...]
     none = jnp.zeros((MODES, WIDTH), jnp.bfloat16)
     highs = jnp.concatenate([jnp.where(mask_of(f, MODES), high, none) for f in range(FLAT)])
-    lows = jnp.concatenate([jnp.where(mask_of(f, MODES), low, none) for f in range(FLAT)])
     y_high, y_low = jnp.concatenate([y_high] * FLAT), jnp.concatenate([y_low] * FLAT)
-    found = dot(highs, y_high) + dot(lows, y_high) + dot(highs, y_low)
+    found = dot(highs, y_high) + dot(highs, y_low)
     row = lax.broadcasted_iota(jnp.int32, (WIDTH, MODES), 0)
     mode = lax.broadcasted_iota(jnp.int32, (WIDTH, MODES), 1)
     gather = (row % MODES == mode).astype(jnp.bfloat16)
@@ -178,7 +175,7 @@
         copies.append(pltpu.make_async_copy(blocks.at[f], out.at[f // 2, f % 2], sems.at[f]))
         copies[-1].start()
         if f == SPECTRA_AFTER:
-            coeffs = dot(highs, gather) + dot(lows, gather)
+            coeffs = dot(highs, gather)
             for g in range(FLAT):
                 modes[g // 2, g % 2] = coeffs[g * MODES : (g + 1) * MODES]
             copies.append(pltpu.make_async_copy(modes, spectra, sems.at[FLAT]))

time: 35.5 us -> 35 us (0.986)
  Pallas kernels: 5.71 us -> 5.33 us
    pallas_call x1, Pallas kernels: 3 us -> 2.64 us  [per_device(): pl.pallas_call(synthesise, out_shape=(jax.ShapeDtypeStruct((4, 2, cols_x,...]
    ppermute x3 -> x2, waiting for transfers between devices: 2.07 us -> 1.83 us  [the longest x1 1.06 us: total_of(): lax.ppermute(value, AXES, hand_over(core, LAST)).astype(jnp.float32)]
    ppermute x3 -> x2, starting transfers between devices: 3.87 us -> 4 us  [the longest x1 2.74 us: total_of(): other = lax.ppermute(total, AXES, swap_cores())]
    ppermute x3 -> x4, starting transfers between devices: 1.77 us -> 1.76 us  [total_of(): own = lax.ppermute(value, AXES, swap_cores()).astype(jnp.float32)]
  transfers between devices with their start and end apart: 16 -> 16, of which waited for: 8 -> 10; matrix products, arithmetic and copies ran while one was open for 0% -> 0% of each run, Pallas kernels for 0% -> 0%
where the time goes in v4:
time: 35 us; the launch traced here: 34.9 us
  starting transfers between devices  18.1 us (52%)
  waiting for transfers between devices  10.6 us (30%)
  Pallas kernels  5.33 us (15%)
  between operations  0.7 us (2%)
    ppermute x9, starting transfers between devices, total_of(): lax.ppermute(value, AXES, hand_over(core, move)).astype(jnp.float32)  8.97 us
    ppermute x9, waiting for transfers between devices, total_of(): lax.ppermute(value, AXES, hand_over(core, move)).astype(jnp.float32)  7.72 us
    ppermute x1, starting transfers between devices, total_of(): lax.ppermute(half, AXES, swap_cores()).astype(jnp.float32)  3.33 us
    ppermute x1, starting transfers between devices, total_of(): other = lax.ppermute(total, AXES, swap_cores())  2.74 us
    pallas_call x1, Pallas kernels, per_device(): pl.pallas_call(lambda *refs: analyse(scale, *refs), out_shape=(small, jax...  2.69 us
    pallas_call x1, Pallas kernels, per_device(): pl.pallas_call(synthesise, out_shape=(jax.ShapeDtypeStruct((4, 2, cols_x,...  2.64 us
    ppermute x4, starting transfers between devices, total_of(): own = lax.ppermute(value, AXES, swap_cores()).astype(jnp.float32)  1.76 us
    ppermute x1, starting transfers between devices, total_of(): lax.ppermute(value, AXES, hand_over(core, LAST)).astype(jnp.float32)  1.26 us
  transfers between devices with their start and end apart: 16, of which 10 were waited for; matrix products, arithmetic and copies ran while one was open for 0% of the time, Pallas kernels for 0%

profile of v4, /device:TPU:1, one launch (start us, length us, event | category | flops | bytes accessed | tf_op | source)
XLA Modules:
  0.0 34.9 jit_solution(11289206629389792225)
XLA Ops:
  0.6 0.0 copy-start.1
  0.6 0.0 copy-start
  0.6 2.7 %analyse.1 = (bf16[48,384]{1,0:T(8,128)(2,1)S(1)}, bf16[768,144]{1,0:T(8,128)(2,1)S(1)}, bf16[96,256]{1,0:T(8,128)(2,1)S(1)}) custom-call(bf16[4,2,768,256]{3,2,1,0:T(8,128)(2,1)} %refs_0_.1, bf16[8,256,768]{2,1,0:T(8,128)(2,1)} %constant.14.clone.refs_1_, bf16[32,192,256]{2,1,0:T(8,128)(2,1)} %constant.15.clone.refs_2_, ...), custom_call_target="tpu_custom_call" | custom-call | tf_op jit(solution)/shard_map/analyse/pallas_call | solution.py:205
  3.3 3.3 %collective-permute-start = (bf16[48,384]{1,0:T(8,128)(2,1)S(1)}, bf16[48,384]{1,0:T(8,128)(2,1)S(1)}, u32[]{:S(2)}, u32[]{:S(2)}) collective-permute-start(bf16[48,384]{1,0:T(8,128)(2,1)S(1)} %get-tuple-element.5), channel_id=1, source_target_pairs={{0,32},{32,0},{4,36},{36,4},{8,40},{40,8},{12,44},{44,12},{16,48},... | collective-permute-start | bytes 110600 | tf_op jit(solution)/shard_map/total/ppermute | solution.py:81
  6.7 0.9 %collective-permute-done = bf16[48,384]{1,0:T(8,128)(2,1)S(1)} collective-permute-done((bf16[48,384]{1,0:T(8,128)(2,1)S(1)}, bf16[48,384]{1,0:T(8,128)(2,1)S(1)}, u32[]{:S(2)}, u32[]{:S(2)}) %collective-permute-start) | collective-permute-done | bytes 36896 | tf_op jit(solution)/shard_map/total/ppermute | solution.py:81
  7.6 0.4 %collective-permute-start.4 = (bf16[48,384]{1,0:T(8,128)(2,1)S(1)}, bf16[48,384]{1,0:T(8,128)(2,1)S(1)}, u32[]{:S(2)}, u32[]{:S(2)}) collective-permute-start(bf16[48,384]{1,0:T(8,128)(2,1)S(1)} %add_convert_fusion.4), channel_id=1, source_target_pairs={{0,97},{32,0},{4,101},{36,4},{8,105},{40,8},{12,109},{44,12},{16,1... | collective-permute-start | bytes 110600 | tf_op jit(solution)/shard_map/total/ppermute | solution.py:85
  8.0 0.5 %collective-permute-start.3 = (bf16[48,384]{1,0:T(8,128)(2,1)S(1)}, bf16[48,384]{1,0:T(8,128)(2,1)S(1)}, u32[]{:S(2)}, u32[]{:S(2)}) collective-permute-start(bf16[48,384]{1,0:T(8,128)(2,1)S(1)} %add_convert_fusion.4), channel_id=1, source_target_pairs={{0,33},{32,0},{4,37},{36,4},{8,41},{40,8},{12,45},{44,12},{16,49},... | collective-permute-start | bytes 110600 | tf_op jit(solution)/shard_map/total/ppermute | solution.py:85
  8.5 0.0 collective-permute-start.2
  8.5 0.6 %collective-permute-start.1 = (bf16[48,384]{1,0:T(8,128)(2,1)S(1)}, bf16[48,384]{1,0:T(8,128)(2,1)S(1)}, u32[]{:S(2)}, u32[]{:S(2)}) collective-permute-start(bf16[48,384]{1,0:T(8,128)(2,1)S(1)} %add_convert_fusion.4), channel_id=1, source_target_pairs={{0,32},{32,0},{4,36},{36,4},{8,40},{40,8},{12,44},{44,12},{16,48},... | collective-permute-start | bytes 110600 | tf_op jit(solution)/shard_map/total/ppermute | solution.py:88
  9.2 2.8 %collective-permute-done.4 = bf16[48,384]{1,0:T(8,128)(2,1)S(1)} collective-permute-done((bf16[48,384]{1,0:T(8,128)(2,1)S(1)}, bf16[48,384]{1,0:T(8,128)(2,1)S(1)}, u32[]{:S(2)}, u32[]{:S(2)}) %collective-permute-start.4) | collective-permute-done | bytes 36896 | tf_op jit(solution)/shard_map/total/ppermute | solution.py:85
  11.9 0.0 collective-permute-done.3
  11.9 0.0 collective-permute-done.2
  11.9 0.0 collective-permute-done.1
  12.0 3.2 %collective-permute-start.8 = (bf16[48,384]{1,0:T(8,128)(2,1)S(1)}, bf16[48,384]{1,0:T(8,128)(2,1)S(1)}, u32[]{:S(2)}, u32[]{:S(2)}) collective-permute-start(bf16[48,384]{1,0:T(8,128)(2,1)S(1)} %add_convert_fusion.3), channel_id=1, source_target_pairs={{32,12},{0,32},{36,8},{4,36},{40,4},{8,40},{44,0},{12,44},{48,28},... | collective-permute-start | bytes 110600 | tf_op jit(solution)/shard_map/total/ppermute | solution.py:85
  15.1 0.3 collective-permute-start.7
  15.4 0.0 collective-permute-start.6
  15.4 0.5 %collective-permute-start.5 = (bf16[48,384]{1,0:T(8,128)(2,1)S(1)}, bf16[48,384]{1,0:T(8,128)(2,1)S(1)}, u32[]{:S(2)}, u32[]{:S(2)}) collective-permute-start(bf16[48,384]{1,0:T(8,128)(2,1)S(1)} %add_convert_fusion.3), channel_id=1, source_target_pairs={{0,32},{32,0},{4,36},{36,4},{8,40},{40,8},{12,44},{44,12},{16,48},... | collective-permute-start | bytes 110600 | tf_op jit(solution)/shard_map/total/ppermute | solution.py:88
  15.9 0.3 collective-permute-done.8
  16.2 0.3 collective-permute-done.7
  16.5 0.3 collective-permute-done.6
  16.9 0.0 collective-permute-done.5
  16.9 2.3 %collective-permute-start.12 = (bf16[48,384]{1,0:T(8,128)(2,1)S(1)}, bf16[48,384]{1,0:T(8,128)(2,1)S(1)}, u32[]{:S(2)}, u32[]{:S(2)}) collective-permute-start(bf16[48,384]{1,0:T(8,128)(2,1)S(1)} %add_convert_fusion.2), channel_id=1, source_target_pairs={{0,227},{32,0},{4,231},{36,4},{8,235},{40,8},{12,239},{44,12},{16,... | collective-permute-start | bytes 110600 | tf_op jit(solution)/shard_map/total/ppermute | solution.py:85
  19.2 2.3 %collective-permute-start.11 = (bf16[48,384]{1,0:T(8,128)(2,1)S(1)}, bf16[48,384]{1,0:T(8,128)(2,1)S(1)}, u32[]{:S(2)}, u32[]{:S(2)}) collective-permute-start(bf16[48,384]{1,0:T(8,128)(2,1)S(1)} %add_convert_fusion.2), channel_id=1, source_target_pairs={{0,35},{32,0},{4,39},{36,4},{8,43},{40,8},{12,47},{44,12},{16,51},... | collective-permute-start | bytes 110600 | tf_op jit(solution)/shard_map/total/ppermute | solution.py:85
  21.5 0.0 collective-permute-start.10
  21.5 0.6 %collective-permute-start.9 = (bf16[48,384]{1,0:T(8,128)(2,1)S(1)}, bf16[48,384]{1,0:T(8,128)(2,1)S(1)}, u32[]{:S(2)}, u32[]{:S(2)}) collective-permute-start(bf16[48,384]{1,0:T(8,128)(2,1)S(1)} %add_convert_fusion.2), channel_id=1, source_target_pairs={{0,32},{32,0},{4,36},{36,4},{8,40},{40,8},{12,44},{44,12},{16,48},... | collective-permute-start | bytes 110600 | tf_op jit(solution)/shard_map/total/ppermute | solution.py:88
  22.1 2.7 %collective-permute-done.12 = bf16[48,384]{1,0:T(8,128)(2,1)S(1)} collective-permute-done((bf16[48,384]{1,0:T(8,128)(2,1)S(1)}, bf16[48,384]{1,0:T(8,128)(2,1)S(1)}, u32[]{:S(2)}, u32[]{:S(2)}) %collective-permute-start.12) | collective-permute-done | bytes 36896 | tf_op jit(solution)/shard_map/total/ppermute | solution.py:85
  24.8 0.0 collective-permute-done.11
  24.8 1.3 %collective-permute-done.10 = bf16[48,384]{1,0:T(8,128)(2,1)S(1)} collective-permute-done((bf16[48,384]{1,0:T(8,128)(2,1)S(1)}, bf16[48,384]{1,0:T(8,128)(2,1)S(1)}, u32[]{:S(2)}, u32[]{:S(2)}) %collective-permute-start.10) | collective-permute-done | bytes 36896 | tf_op jit(solution)/shard_map/total/ppermute | solution.py:85
  26.1 0.0 collective-permute-done.9
  26.1 1.3 %collective-permute-start.14 = (bf16[48,384]{1,0:T(8,128)(2,1)S(1)}, bf16[48,384]{1,0:T(8,128)(2,1)S(1)}, u32[]{:S(2)}, u32[]{:S(2)}) collective-permute-start(bf16[48,384]{1,0:T(8,128)(2,1)S(1)} %add_convert_fusion.1), channel_id=1, source_target_pairs={{32,28},{0,32},{36,24},{4,36},{40,20},{8,40},{44,16},{12,44},{48,1... | collective-permute-start | bytes 110600 | tf_op jit(solution)/shard_map/total/ppermute | solution.py:92
  27.4 0.0 collective-permute-start.13
  27.4 1.1 %collective-permute-done.14 = bf16[48,384]{1,0:T(8,128)(2,1)S(1)} collective-permute-done((bf16[48,384]{1,0:T(8,128)(2,1)S(1)}, bf16[48,384]{1,0:T(8,128)(2,1)S(1)}, u32[]{:S(2)}, u32[]{:S(2)}) %collective-permute-start.14) | collective-permute-done | bytes 36896 | tf_op jit(solution)/shard_map/total/ppermute | solution.py:92
  28.4 0.2 collective-permute-done.13
  28.6 2.7 %collective-permute-start.15 = (bf16[48,384]{1,0:T(8,128)(2,1)S(1)}, bf16[48,384]{1,0:T(8,128)(2,1)S(1)}, u32[]{:S(2)}, u32[]{:S(2)}) collective-permute-start(bf16[48,384]{1,0:T(8,128)(2,1)S(1)} %add_convert_fusion), channel_id=1, source_target_pairs={{0,32},{32,0},{4,36},{36,4},{8,40},{40,8},{12,44},{44,12},{16,48},... | collective-permute-start | bytes 110600 | tf_op jit(solution)/shard_map/total/ppermute | solution.py:95
  31.3 0.0 copy-done.1
  31.3 0.1 copy.8.rate
  31.4 0.8 %collective-permute-done.15 = bf16[48,384]{1,0:T(8,128)(2,1)S(1)} collective-permute-done((bf16[48,384]{1,0:T(8,128)(2,1)S(1)}, bf16[48,384]{1,0:T(8,128)(2,1)S(1)}, u32[]{:S(2)}, u32[]{:S(2)}) %collective-permute-start.15) | collective-permute-done | bytes 36896 | tf_op jit(solution)/shard_map/total/ppermute | solution.py:95
  32.2 0.0 copy-done
  32.2 2.6 %synthesise.1 = (bf16[4,2,768,256]{3,2,1,0:T(8,128)(2,1)}, f32[4,2,48,48]{3,2,1,0:T(8,128)}) custom-call(bf16[48,384]{1,0:T(8,128)(2,1)S(1)} %broadcast_select_fusion.sums, f32[4,2,48,48]{3,2,1,0:T(8,128)S(1)} %copy-done, f32[4,2]{1,0:T(4,128)S(1)} %copy.8.rate, bf16[768,144]{1,0:T(8,128)(2,1)S(1)} %get-tuple-element.6.x_table, ...), custom_call_target="tpu_custom_call" | custom-call | tf_op jit(solution)/shard_map/synthesise/pallas_call | solution.py:226
  (6 shorter events, 0.1 us)
Async XLA Ops:
  0.6 30.7 %copy-start.1 = (f32[4,2]{0,1:T(2,128)S(1)}, f32[4,2]{0,1:T(2,128)}, u32[]{:S(2)}) copy-start(f32[4,2]{0,1:T(2,128)} %param.8) | copy-start | bytes 100
  0.6 31.6 %copy-start = (f32[4,2,48,48]{3,2,1,0:T(8,128)S(1)}, f32[4,2,48,48]{3,2,1,0:T(8,128)}, u32[]{:S(2)}) copy-start(f32[4,2,48,48]{3,2,1,0:T(8,128)} %parent.1) | copy-start | bytes 221188
  3.3 4.2 %collective-permute-start = (bf16[48,384]{1,0:T(8,128)(2,1)S(1)}, bf16[48,384]{1,0:T(8,128)(2,1)S(1)}, u32[]{:S(2)}, u32[]{:S(2)}) collective-permute-start(bf16[48,384]{1,0:T(8,128)(2,1)S(1)} %get-tuple-element.5), channel_id=1, source_target_pairs={{0,32},{32,0},{4,36},{36,4},{8,40},{40,8},{12,44},{44,12},{16,48},... | collective-permute-start | bytes 110600 | tf_op jit(solution)/shard_map/total/ppermute | solution.py:81
  7.6 4.4 %collective-permute-start.4 = (bf16[48,384]{1,0:T(8,128)(2,1)S(1)}, bf16[48,384]{1,0:T(8,128)(2,1)S(1)}, u32[]{:S(2)}, u32[]{:S(2)}) collective-permute-start(bf16[48,384]{1,0:T(8,128)(2,1)S(1)} %add_convert_fusion.4), channel_id=1, source_target_pairs={{0,97},{32,0},{4,101},{36,4},{8,105},{40,8},{12,109},{44,12},{16,1... | collective-permute-start | bytes 110600 | tf_op jit(solution)/shard_map/total/ppermute | solution.py:85
  8.0 3.9 %collective-permute-start.3 = (bf16[48,384]{1,0:T(8,128)(2,1)S(1)}, bf16[48,384]{1,0:T(8,128)(2,1)S(1)}, u32[]{:S(2)}, u32[]{:S(2)}) collective-permute-start(bf16[48,384]{1,0:T(8,128)(2,1)S(1)} %add_convert_fusion.4), channel_id=1, source_target_pairs={{0,33},{32,0},{4,37},{36,4},{8,41},{40,8},{12,45},{44,12},{16,49},... | collective-permute-start | bytes 110600 | tf_op jit(solution)/shard_map/total/ppermute | solution.py:85
  8.5 3.4 %collective-permute-start.2 = (bf16[48,384]{1,0:T(8,128)(2,1)S(1)}, bf16[48,384]{1,0:T(8,128)(2,1)S(1)}, u32[]{:S(2)}, u32[]{:S(2)}) collective-permute-start(bf16[48,384]{1,0:T(8,128)(2,1)S(1)} %add_convert_fusion.4), channel_id=1, source_target_pairs={{0,96},{32,0},{4,100},{36,4},{8,104},{40,8},{12,108},{44,12},{16,1... | collective-permute-start | bytes 110600 | tf_op jit(solution)/shard_map/total/ppermute | solution.py:85
  8.5 3.4 %collective-permute-start.1 = (bf16[48,384]{1,0:T(8,128)(2,1)S(1)}, bf16[48,384]{1,0:T(8,128)(2,1)S(1)}, u32[]{:S(2)}, u32[]{:S(2)}) collective-permute-start(bf16[48,384]{1,0:T(8,128)(2,1)S(1)} %add_convert_fusion.4), channel_id=1, source_target_pairs={{0,32},{32,0},{4,36},{36,4},{8,40},{40,8},{12,44},{44,12},{16,48},... | collective-permute-start | bytes 110600 | tf_op jit(solution)/shard_map/total/ppermute | solution.py:88
  12.0 4.2 %collective-permute-start.8 = (bf16[48,384]{1,0:T(8,128)(2,1)S(1)}, bf16[48,384]{1,0:T(8,128)(2,1)S(1)}, u32[]{:S(2)}, u32[]{:S(2)}) collective-permute-start(bf16[48,384]{1,0:T(8,128)(2,1)S(1)} %add_convert_fusion.3), channel_id=1, source_target_pairs={{32,12},{0,32},{36,8},{4,36},{40,4},{8,40},{44,0},{12,44},{48,28},... | collective-permute-start | bytes 110600 | tf_op jit(solution)/shard_map/total/ppermute | solution.py:85
  15.1 1.4 %collective-permute-start.7 = (bf16[48,384]{1,0:T(8,128)(2,1)S(1)}, bf16[48,384]{1,0:T(8,128)(2,1)S(1)}, u32[]{:S(2)}, u32[]{:S(2)}) collective-permute-start(bf16[48,384]{1,0:T(8,128)(2,1)S(1)} %add_convert_fusion.3), channel_id=1, source_target_pairs={{32,8},{0,32},{36,12},{4,36},{40,0},{8,40},{44,4},{12,44},{48,24},... | collective-permute-start | bytes 110600 | tf_op jit(solution)/shard_map/total/ppermute | solution.py:85
  15.4 1.5 %collective-permute-start.6 = (bf16[48,384]{1,0:T(8,128)(2,1)S(1)}, bf16[48,384]{1,0:T(8,128)(2,1)S(1)}, u32[]{:S(2)}, u32[]{:S(2)}) collective-permute-start(bf16[48,384]{1,0:T(8,128)(2,1)S(1)} %add_convert_fusion.3), channel_id=1, source_target_pairs={{32,4},{0,32},{36,0},{4,36},{40,12},{8,40},{44,8},{12,44},{48,20},... | collective-permute-start | bytes 110600 | tf_op jit(solution)/shard_map/total/ppermute | solution.py:85
  15.4 1.5 %collective-permute-start.5 = (bf16[48,384]{1,0:T(8,128)(2,1)S(1)}, bf16[48,384]{1,0:T(8,128)(2,1)S(1)}, u32[]{:S(2)}, u32[]{:S(2)}) collective-permute-start(bf16[48,384]{1,0:T(8,128)(2,1)S(1)} %add_convert_fusion.3), channel_id=1, source_target_pairs={{0,32},{32,0},{4,36},{36,4},{8,40},{40,8},{12,44},{44,12},{16,48},... | collective-permute-start | bytes 110600 | tf_op jit(solution)/shard_map/total/ppermute | solution.py:88
  16.9 7.8 %collective-permute-start.12 = (bf16[48,384]{1,0:T(8,128)(2,1)S(1)}, bf16[48,384]{1,0:T(8,128)(2,1)S(1)}, u32[]{:S(2)}, u32[]{:S(2)}) collective-permute-start(bf16[48,384]{1,0:T(8,128)(2,1)S(1)} %add_convert_fusion.2), channel_id=1, source_target_pairs={{0,227},{32,0},{4,231},{36,4},{8,235},{40,8},{12,239},{44,12},{16,... | collective-permute-start | bytes 110600 | tf_op jit(solution)/shard_map/total/ppermute | solution.py:85
  19.2 5.6 %collective-permute-start.11 = (bf16[48,384]{1,0:T(8,128)(2,1)S(1)}, bf16[48,384]{1,0:T(8,128)(2,1)S(1)}, u32[]{:S(2)}, u32[]{:S(2)}) collective-permute-start(bf16[48,384]{1,0:T(8,128)(2,1)S(1)} %add_convert_fusion.2), channel_id=1, source_target_pairs={{0,35},{32,0},{4,39},{36,4},{8,43},{40,8},{12,47},{44,12},{16,51},... | collective-permute-start | bytes 110600 | tf_op jit(solution)/shard_map/total/ppermute | solution.py:85
  21.5 4.6 %collective-permute-start.10 = (bf16[48,384]{1,0:T(8,128)(2,1)S(1)}, bf16[48,384]{1,0:T(8,128)(2,1)S(1)}, u32[]{:S(2)}, u32[]{:S(2)}) collective-permute-start(bf16[48,384]{1,0:T(8,128)(2,1)S(1)} %add_convert_fusion.2), channel_id=1, source_target_pairs={{0,224},{32,0},{4,228},{36,4},{8,232},{40,8},{12,236},{44,12},{16,... | collective-permute-start | bytes 110600 | tf_op jit(solution)/shard_map/total/ppermute | solution.py:85
  21.5 4.6 %collective-permute-start.9 = (bf16[48,384]{1,0:T(8,128)(2,1)S(1)}, bf16[48,384]{1,0:T(8,128)(2,1)S(1)}, u32[]{:S(2)}, u32[]{:S(2)}) collective-permute-start(bf16[48,384]{1,0:T(8,128)(2,1)S(1)} %add_convert_fusion.2), channel_id=1, source_target_pairs={{0,32},{32,0},{4,36},{36,4},{8,40},{40,8},{12,44},{44,12},{16,48},... | collective-permute-start | bytes 110600 | tf_op jit(solution)/shard_map/total/ppermute | solution.py:88
  26.1 2.3 %collective-permute-start.14 = (bf16[48,384]{1,0:T(8,128)(2,1)S(1)}, bf16[48,384]{1,0:T(8,128)(2,1)S(1)}, u32[]{:S(2)}, u32[]{:S(2)}) collective-permute-start(bf16[48,384]{1,0:T(8,128)(2,1)S(1)} %add_convert_fusion.1), channel_id=1, source_target_pairs={{32,28},{0,32},{36,24},{4,36},{40,20},{8,40},{44,16},{12,44},{48,1... | collective-permute-start | bytes 110600 | tf_op jit(solution)/shard_map/total/ppermute | solution.py:92
  27.4 1.2 %collective-permute-start.13 = (bf16[48,384]{1,0:T(8,128)(2,1)S(1)}, bf16[48,384]{1,0:T(8,128)(2,1)S(1)}, u32[]{:S(2)}, u32[]{:S(2)}) collective-permute-start(bf16[48,384]{1,0:T(8,128)(2,1)S(1)} %add_convert_fusion.1), channel_id=1, source_target_pairs={{0,32},{32,0},{4,36},{36,4},{8,40},{40,8},{12,44},{44,12},{16,48},... | collective-permute-start | bytes 110600 | tf_op jit(solution)/shard_map/total/ppermute | solution.py:93
  28.6 3.6 %collective-permute-start.15 = (bf16[48,384]{1,0:T(8,128)(2,1)S(1)}, bf16[48,384]{1,0:T(8,128)(2,1)S(1)}, u32[]{:S(2)}, u32[]{:S(2)}) collective-permute-start(bf16[48,384]{1,0:T(8,128)(2,1)S(1)} %add_convert_fusion), channel_id=1, source_target_pairs={{0,32},{32,0},{4,36},{36,4},{8,40},{40,8},{12,44},{44,12},{16,48},... | collective-permute-start | bytes 110600 | tf_op jit(solution)/shard_map/total/ppermute | solution.py:95

commit v5 on v4

--- a/solution.py
+++ b/solution.py
@@ -134,8 +134,7 @@
         copy.start()
     copy_wide.start()
     copy_y.wait()
-    y_high = jnp.concatenate([y_table[:MODES]] * FLAT)
-    y_low = jnp.concatenate([y_table[MODES:]] * FLAT)
+    y_high, y_low = y_table[:MODES], y_table[MODES:]
     copy_x.wait()
     for pair in range(0, FLAT, 2):
         copies[pair // 2].wait()
@@ -146,9 +145,7 @@
     product = (
         dot(high[...], y_high, last) + dot(low[...], y_high, last) + dot(high[...], y_low, last)
     )
-    total = jnp.zeros((MODES, WIDTH), jnp.float32)
-    for f in range(FLAT):
-        total = jnp.where(mask_of(f, MODES), product[f * MODES : (f + 1) * MODES], total)
+    total = jnp.concatenate([product[f * MODES : (f + 1) * MODES] for f in range(FLAT)], 1)
     out[...] = (total * scale).astype(jnp.bfloat16)
     copy_wide.wait()
 

time: 35 us -> 34.9 us (level)
  no operation moved by 1% of the time
where the time goes in v5:
time: 34.9 us; the launch traced here: 34.8 us
  starting transfers between devices  18.1 us (52%)
  waiting for transfers between devices  10.6 us (30%)
  Pallas kernels  5.23 us (15%)
  between operations  0.7 us (2%)
    ppermute x9, starting transfers between devices, total_of(): lax.ppermute(value, AXES, hand_over(core, move)).astype(jnp.float32)  8.97 us
    ppermute x9, waiting for transfers between devices, total_of(): lax.ppermute(value, AXES, hand_over(core, move)).astype(jnp.float32)  7.71 us
    ppermute x1, starting transfers between devices, total_of(): lax.ppermute(half, AXES, swap_cores()).astype(jnp.float32)  3.33 us
    ppermute x1, starting transfers between devices, total_of(): other = lax.ppermute(total, AXES, swap_cores())  2.73 us
    pallas_call x1, Pallas kernels, per_device(): pl.pallas_call(synthesise, out_shape=(jax.ShapeDtypeStruct((4, 2, cols_x,...  2.65 us
    pallas_call x1, Pallas kernels, per_device(): pl.pallas_call(lambda *refs: analyse(scale, *refs), out_shape=(small, jax...  2.58 us
    ppermute x4, starting transfers between devices, total_of(): own = lax.ppermute(value, AXES, swap_cores()).astype(jnp.float32)  1.77 us
    ppermute x1, starting transfers between devices, total_of(): lax.ppermute(value, AXES, hand_over(core, LAST)).astype(jnp.float32)  1.26 us
  transfers between devices with their start and end apart: 16, of which 10 were waited for; matrix products, arithmetic and copies ran while one was open for 0% of the time, Pallas kernels for 0%

profile of v5, /device:TPU:1, one launch (start us, length us, event | category | flops | bytes accessed | tf_op | source)
XLA Modules:
  0.0 34.8 jit_solution(6876690303278045966)
XLA Ops:
  0.6 0.0 copy-start.1
  0.6 0.0 copy-start
  0.6 2.6 %analyse.1 = (bf16[48,384]{1,0:T(8,128)(2,1)S(1)}, bf16[768,144]{1,0:T(8,128)(2,1)S(1)}, bf16[96,256]{1,0:T(8,128)(2,1)S(1)}) custom-call(bf16[4,2,768,256]{3,2,1,0:T(8,128)(2,1)} %refs_0_.1, bf16[8,256,768]{2,1,0:T(8,128)(2,1)} %constant.14.clone.refs_1_, bf16[32,192,256]{2,1,0:T(8,128)(2,1)} %constant.15.clone.refs_2_, ...), custom_call_target="tpu_custom_call" | custom-call | tf_op jit(solution)/shard_map/analyse/pallas_call | solution.py:202
  3.2 3.3 %collective-permute-start = (bf16[48,384]{1,0:T(8,128)(2,1)S(1)}, bf16[48,384]{1,0:T(8,128)(2,1)S(1)}, u32[]{:S(2)}, u32[]{:S(2)}) collective-permute-start(bf16[48,384]{1,0:T(8,128)(2,1)S(1)} %get-tuple-element.5), channel_id=1, source_target_pairs={{0,32},{32,0},{4,36},{36,4},{8,40},{40,8},{12,44},{44,12},{16,48},... | collective-permute-start | bytes 110600 | tf_op jit(solution)/shard_map/total/ppermute | solution.py:81
  6.6 0.9 %collective-permute-done = bf16[48,384]{1,0:T(8,128)(2,1)S(1)} collective-permute-done((bf16[48,384]{1,0:T(8,128)(2,1)S(1)}, bf16[48,384]{1,0:T(8,128)(2,1)S(1)}, u32[]{:S(2)}, u32[]{:S(2)}) %collective-permute-start) | collective-permute-done | bytes 36896 | tf_op jit(solution)/shard_map/total/ppermute | solution.py:81
  7.4 0.4 %collective-permute-start.4 = (bf16[48,384]{1,0:T(8,128)(2,1)S(1)}, bf16[48,384]{1,0:T(8,128)(2,1)S(1)}, u32[]{:S(2)}, u32[]{:S(2)}) collective-permute-start(bf16[48,384]{1,0:T(8,128)(2,1)S(1)} %add_convert_fusion.4), channel_id=1, source_target_pairs={{0,97},{32,0},{4,101},{36,4},{8,105},{40,8},{12,109},{44,12},{16,1... | collective-permute-start | bytes 110600 | tf_op jit(solution)/shard_map/total/ppermute | solution.py:85
  7.9 0.5 %collective-permute-start.3 = (bf16[48,384]{1,0:T(8,128)(2,1)S(1)}, bf16[48,384]{1,0:T(8,128)(2,1)S(1)}, u32[]{:S(2)}, u32[]{:S(2)}) collective-permute-start(bf16[48,384]{1,0:T(8,128)(2,1)S(1)} %add_convert_fusion.4), channel_id=1, source_target_pairs={{0,33},{32,0},{4,37},{36,4},{8,41},{40,8},{12,45},{44,12},{16,49},... | collective-permute-start | bytes 110600 | tf_op jit(solution)/shard_map/total/ppermute | solution.py:85
  8.4 0.0 collective-permute-start.2
  8.4 0.6 %collective-permute-start.1 = (bf16[48,384]{1,0:T(8,128)(2,1)S(1)}, bf16[48,384]{1,0:T(8,128)(2,1)S(1)}, u32[]{:S(2)}, u32[]{:S(2)}) collective-permute-start(bf16[48,384]{1,0:T(8,128)(2,1)S(1)} %add_convert_fusion.4), channel_id=1, source_target_pairs={{0,32},{32,0},{4,36},{36,4},{8,40},{40,8},{12,44},{44,12},{16,48},... | collective-permute-start | bytes 110600 | tf_op jit(solution)/shard_map/total/ppermute | solution.py:88
  9.1 2.7 %collective-permute-done.4 = bf16[48,384]{1,0:T(8,128)(2,1)S(1)} collective-permute-done((bf16[48,384]{1,0:T(8,128)(2,1)S(1)}, bf16[48,384]{1,0:T(8,128)(2,1)S(1)}, u32[]{:S(2)}, u32[]{:S(2)}) %collective-permute-start.4) | collective-permute-done | bytes 36896 | tf_op jit(solution)/shard_map/total/ppermute | solution.py:85
  11.8 0.0 collective-permute-done.3
  11.8 0.0 collective-permute-done.2
  11.8 0.0 collective-permute-done.1
  11.9 3.2 %collective-permute-start.8 = (bf16[48,384]{1,0:T(8,128)(2,1)S(1)}, bf16[48,384]{1,0:T(8,128)(2,1)S(1)}, u32[]{:S(2)}, u32[]{:S(2)}) collective-permute-start(bf16[48,384]{1,0:T(8,128)(2,1)S(1)} %add_convert_fusion.3), channel_id=1, source_target_pairs={{32,12},{0,32},{36,8},{4,36},{40,4},{8,40},{44,0},{12,44},{48,28},... | collective-permute-start | bytes 110600 | tf_op jit(solution)/shard_map/total/ppermute | solution.py:85
  15.0 0.3 collective-permute-start.7
  15.3 0.0 collective-permute-start.6
  15.3 0.5 %collective-permute-start.5 = (bf16[48,384]{1,0:T(8,128)(2,1)S(1)}, bf16[48,384]{1,0:T(8,128)(2,1)S(1)}, u32[]{:S(2)}, u32[]{:S(2)}) collective-permute-start(bf16[48,384]{1,0:T(8,128)(2,1)S(1)} %add_convert_fusion.3), channel_id=1, source_target_pairs={{0,32},{32,0},{4,36},{36,4},{8,40},{40,8},{12,44},{44,12},{16,48},... | collective-permute-start | bytes 110600 | tf_op jit(solution)/shard_map/total/ppermute | solution.py:88
  15.8 0.3 collective-permute-done.8
  16.1 0.3 collective-permute-done.7
  16.4 0.3 collective-permute-done.6
  16.8 0.0 collective-permute-done.5
  16.8 2.3 %collective-permute-start.12 = (bf16[48,384]{1,0:T(8,128)(2,1)S(1)}, bf16[48,384]{1,0:T(8,128)(2,1)S(1)}, u32[]{:S(2)}, u32[]{:S(2)}) collective-permute-start(bf16[48,384]{1,0:T(8,128)(2,1)S(1)} %add_convert_fusion.2), channel_id=1, source_target_pairs={{0,227},{32,0},{4,231},{36,4},{8,235},{40,8},{12,239},{44,12},{16,... | collective-permute-start | bytes 110600 | tf_op jit(solution)/shard_map/total/ppermute | solution.py:85
  19.1 2.3 %collective-permute-start.11 = (bf16[48,384]{1,0:T(8,128)(2,1)S(1)}, bf16[48,384]{1,0:T(8,128)(2,1)S(1)}, u32[]{:S(2)}, u32[]{:S(2)}) collective-permute-start(bf16[48,384]{1,0:T(8,128)(2,1)S(1)} %add_convert_fusion.2), channel_id=1, source_target_pairs={{0,35},{32,0},{4,39},{36,4},{8,43},{40,8},{12,47},{44,12},{16,51},... | collective-permute-start | bytes 110600 | tf_op jit(solution)/shard_map/total/ppermute | solution.py:85
  21.4 0.0 collective-permute-start.10
  21.4 0.6 %collective-permute-start.9 = (bf16[48,384]{1,0:T(8,128)(2,1)S(1)}, bf16[48,384]{1,0:T(8,128)(2,1)S(1)}, u32[]{:S(2)}, u32[]{:S(2)}) collective-permute-start(bf16[48,384]{1,0:T(8,128)(2,1)S(1)} %add_convert_fusion.2), channel_id=1, source_target_pairs={{0,32},{32,0},{4,36},{36,4},{8,40},{40,8},{12,44},{44,12},{16,48},... | collective-permute-start | bytes 110600 | tf_op jit(solution)/shard_map/total/ppermute | solution.py:88
  22.0 2.7 %collective-permute-done.12 = bf16[48,384]{1,0:T(8,128)(2,1)S(1)} collective-permute-done((bf16[48,384]{1,0:T(8,128)(2,1)S(1)}, bf16[48,384]{1,0:T(8,128)(2,1)S(1)}, u32[]{:S(2)}, u32[]{:S(2)}) %collective-permute-start.12) | collective-permute-done | bytes 36896 | tf_op jit(solution)/shard_map/total/ppermute | solution.py:85
  24.7 0.0 collective-permute-done.11
  24.7 1.3 %collective-permute-done.10 = bf16[48,384]{1,0:T(8,128)(2,1)S(1)} collective-permute-done((bf16[48,384]{1,0:T(8,128)(2,1)S(1)}, bf16[48,384]{1,0:T(8,128)(2,1)S(1)}, u32[]{:S(2)}, u32[]{:S(2)}) %collective-permute-start.10) | collective-permute-done | bytes 36896 | tf_op jit(solution)/shard_map/total/ppermute | solution.py:85
  26.0 0.0 collective-permute-done.9
  26.0 1.3 %collective-permute-start.14 = (bf16[48,384]{1,0:T(8,128)(2,1)S(1)}, bf16[48,384]{1,0:T(8,128)(2,1)S(1)}, u32[]{:S(2)}, u32[]{:S(2)}) collective-permute-start(bf16[48,384]{1,0:T(8,128)(2,1)S(1)} %add_convert_fusion.1), channel_id=1, source_target_pairs={{32,28},{0,32},{36,24},{4,36},{40,20},{8,40},{44,16},{12,44},{48,1... | collective-permute-start | bytes 110600 | tf_op jit(solution)/shard_map/total/ppermute | solution.py:92
  27.3 0.0 collective-permute-start.13
  27.3 1.1 %collective-permute-done.14 = bf16[48,384]{1,0:T(8,128)(2,1)S(1)} collective-permute-done((bf16[48,384]{1,0:T(8,128)(2,1)S(1)}, bf16[48,384]{1,0:T(8,128)(2,1)S(1)}, u32[]{:S(2)}, u32[]{:S(2)}) %collective-permute-start.14) | collective-permute-done | bytes 36896 | tf_op jit(solution)/shard_map/total/ppermute | solution.py:92
  28.3 0.2 collective-permute-done.13
  28.5 2.7 %collective-permute-start.15 = (bf16[48,384]{1,0:T(8,128)(2,1)S(1)}, bf16[48,384]{1,0:T(8,128)(2,1)S(1)}, u32[]{:S(2)}, u32[]{:S(2)}) collective-permute-start(bf16[48,384]{1,0:T(8,128)(2,1)S(1)} %add_convert_fusion), channel_id=1, source_target_pairs={{0,32},{32,0},{4,36},{36,4},{8,40},{40,8},{12,44},{44,12},{16,48},... | collective-permute-start | bytes 110600 | tf_op jit(solution)/shard_map/total/ppermute | solution.py:95
  31.2 0.0 copy-done.1
  31.2 0.1 copy.8.rate
  31.3 0.8 %collective-permute-done.15 = bf16[48,384]{1,0:T(8,128)(2,1)S(1)} collective-permute-done((bf16[48,384]{1,0:T(8,128)(2,1)S(1)}, bf16[48,384]{1,0:T(8,128)(2,1)S(1)}, u32[]{:S(2)}, u32[]{:S(2)}) %collective-permute-start.15) | collective-permute-done | bytes 36896 | tf_op jit(solution)/shard_map/total/ppermute | solution.py:95
  32.1 0.0 copy-done
  32.1 2.6 %synthesise.1 = (bf16[4,2,768,256]{3,2,1,0:T(8,128)(2,1)}, f32[4,2,48,48]{3,2,1,0:T(8,128)}) custom-call(bf16[48,384]{1,0:T(8,128)(2,1)S(1)} %broadcast_select_fusion.sums, f32[4,2,48,48]{3,2,1,0:T(8,128)S(1)} %copy-done, f32[4,2]{1,0:T(4,128)S(1)} %copy.8.rate, bf16[768,144]{1,0:T(8,128)(2,1)S(1)} %get-tuple-element.6.x_table, ...), custom_call_target="tpu_custom_call" | custom-call | tf_op jit(solution)/shard_map/synthesise/pallas_call | solution.py:223
  (6 shorter events, 0.1 us)
Async XLA Ops:
  0.6 30.6 %copy-start.1 = (f32[4,2]{0,1:T(2,128)S(1)}, f32[4,2]{0,1:T(2,128)}, u32[]{:S(2)}) copy-start(f32[4,2]{0,1:T(2,128)} %param.8) | copy-start | bytes 100
  0.6 31.5 %copy-start = (f32[4,2,48,48]{3,2,1,0:T(8,128)S(1)}, f32[4,2,48,48]{3,2,1,0:T(8,128)}, u32[]{:S(2)}) copy-start(f32[4,2,48,48]{3,2,1,0:T(8,128)} %parent.1) | copy-start | bytes 221188
  3.2 4.2 %collective-permute-start = (bf16[48,384]{1,0:T(8,128)(2,1)S(1)}, bf16[48,384]{1,0:T(8,128)(2,1)S(1)}, u32[]{:S(2)}, u32[]{:S(2)}) collective-permute-start(bf16[48,384]{1,0:T(8,128)(2,1)S(1)} %get-tuple-element.5), channel_id=1, source_target_pairs={{0,32},{32,0},{4,36},{36,4},{8,40},{40,8},{12,44},{44,12},{16,48},... | collective-permute-start | bytes 110600 | tf_op jit(solution)/shard_map/total/ppermute | solution.py:81
  7.4 4.4 %collective-permute-start.4 = (bf16[48,384]{1,0:T(8,128)(2,1)S(1)}, bf16[48,384]{1,0:T(8,128)(2,1)S(1)}, u32[]{:S(2)}, u32[]{:S(2)}) collective-permute-start(bf16[48,384]{1,0:T(8,128)(2,1)S(1)} %add_convert_fusion.4), channel_id=1, source_target_pairs={{0,97},{32,0},{4,101},{36,4},{8,105},{40,8},{12,109},{44,12},{16,1... | collective-permute-start | bytes 110600 | tf_op jit(solution)/shard_map/total/ppermute | solution.py:85
  7.9 3.9 %collective-permute-start.3 = (bf16[48,384]{1,0:T(8,128)(2,1)S(1)}, bf16[48,384]{1,0:T(8,128)(2,1)S(1)}, u32[]{:S(2)}, u32[]{:S(2)}) collective-permute-start(bf16[48,384]{1,0:T(8,128)(2,1)S(1)} %add_convert_fusion.4), channel_id=1, source_target_pairs={{0,33},{32,0},{4,37},{36,4},{8,41},{40,8},{12,45},{44,12},{16,49},... | collective-permute-start | bytes 110600 | tf_op jit(solution)/shard_map/total/ppermute | solution.py:85
  8.4 3.4 %collective-permute-start.2 = (bf16[48,384]{1,0:T(8,128)(2,1)S(1)}, bf16[48,384]{1,0:T(8,128)(2,1)S(1)}, u32[]{:S(2)}, u32[]{:S(2)}) collective-permute-start(bf16[48,384]{1,0:T(8,128)(2,1)S(1)} %add_convert_fusion.4), channel_id=1, source_target_pairs={{0,96},{32,0},{4,100},{36,4},{8,104},{40,8},{12,108},{44,12},{16,1... | collective-permute-start | bytes 110600 | tf_op jit(solution)/shard_map/total/ppermute | solution.py:85
  8.4 3.4 %collective-permute-start.1 = (bf16[48,384]{1,0:T(8,128)(2,1)S(1)}, bf16[48,384]{1,0:T(8,128)(2,1)S(1)}, u32[]{:S(2)}, u32[]{:S(2)}) collective-permute-start(bf16[48,384]{1,0:T(8,128)(2,1)S(1)} %add_convert_fusion.4), channel_id=1, source_target_pairs={{0,32},{32,0},{4,36},{36,4},{8,40},{40,8},{12,44},{44,12},{16,48},... | collective-permute-start | bytes 110600 | tf_op jit(solution)/shard_map/total/ppermute | solution.py:88
  11.9 4.2 %collective-permute-start.8 = (bf16[48,384]{1,0:T(8,128)(2,1)S(1)}, bf16[48,384]{1,0:T(8,128)(2,1)S(1)}, u32[]{:S(2)}, u32[]{:S(2)}) collective-permute-start(bf16[48,384]{1,0:T(8,128)(2,1)S(1)} %add_convert_fusion.3), channel_id=1, source_target_pairs={{32,12},{0,32},{36,8},{4,36},{40,4},{8,40},{44,0},{12,44},{48,28},... | collective-permute-start | bytes 110600 | tf_op jit(solution)/shard_map/total/ppermute | solution.py:85
  15.0 1.4 %collective-permute-start.7 = (bf16[48,384]{1,0:T(8,128)(2,1)S(1)}, bf16[48,384]{1,0:T(8,128)(2,1)S(1)}, u32[]{:S(2)}, u32[]{:S(2)}) collective-permute-start(bf16[48,384]{1,0:T(8,128)(2,1)S(1)} %add_convert_fusion.3), channel_id=1, source_target_pairs={{32,8},{0,32},{36,12},{4,36},{40,0},{8,40},{44,4},{12,44},{48,24},... | collective-permute-start | bytes 110600 | tf_op jit(solution)/shard_map/total/ppermute | solution.py:85
  15.3 1.5 %collective-permute-start.6 = (bf16[48,384]{1,0:T(8,128)(2,1)S(1)}, bf16[48,384]{1,0:T(8,128)(2,1)S(1)}, u32[]{:S(2)}, u32[]{:S(2)}) collective-permute-start(bf16[48,384]{1,0:T(8,128)(2,1)S(1)} %add_convert_fusion.3), channel_id=1, source_target_pairs={{32,4},{0,32},{36,0},{4,36},{40,12},{8,40},{44,8},{12,44},{48,20},... | collective-permute-start | bytes 110600 | tf_op jit(solution)/shard_map/total/ppermute | solution.py:85
  15.3 1.5 %collective-permute-start.5 = (bf16[48,384]{1,0:T(8,128)(2,1)S(1)}, bf16[48,384]{1,0:T(8,128)(2,1)S(1)}, u32[]{:S(2)}, u32[]{:S(2)}) collective-permute-start(bf16[48,384]{1,0:T(8,128)(2,1)S(1)} %add_convert_fusion.3), channel_id=1, source_target_pairs={{0,32},{32,0},{4,36},{36,4},{8,40},{40,8},{12,44},{44,12},{16,48},... | collective-permute-start | bytes 110600 | tf_op jit(solution)/shard_map/total/ppermute | solution.py:88
  16.8 7.8 %collective-permute-start.12 = (bf16[48,384]{1,0:T(8,128)(2,1)S(1)}, bf16[48,384]{1,0:T(8,128)(2,1)S(1)}, u32[]{:S(2)}, u32[]{:S(2)}) collective-permute-start(bf16[48,384]{1,0:T(8,128)(2,1)S(1)} %add_convert_fusion.2), channel_id=1, source_target_pairs={{0,227},{32,0},{4,231},{36,4},{8,235},{40,8},{12,239},{44,12},{16,... | collective-permute-start | bytes 110600 | tf_op jit(solution)/shard_map/total/ppermute | solution.py:85
  19.1 5.6 %collective-permute-start.11 = (bf16[48,384]{1,0:T(8,128)(2,1)S(1)}, bf16[48,384]{1,0:T(8,128)(2,1)S(1)}, u32[]{:S(2)}, u32[]{:S(2)}) collective-permute-start(bf16[48,384]{1,0:T(8,128)(2,1)S(1)} %add_convert_fusion.2), channel_id=1, source_target_pairs={{0,35},{32,0},{4,39},{36,4},{8,43},{40,8},{12,47},{44,12},{16,51},... | collective-permute-start | bytes 110600 | tf_op jit(solution)/shard_map/total/ppermute | solution.py:85
  21.4 4.6 %collective-permute-start.10 = (bf16[48,384]{1,0:T(8,128)(2,1)S(1)}, bf16[48,384]{1,0:T(8,128)(2,1)S(1)}, u32[]{:S(2)}, u32[]{:S(2)}) collective-permute-start(bf16[48,384]{1,0:T(8,128)(2,1)S(1)} %add_convert_fusion.2), channel_id=1, source_target_pairs={{0,224},{32,0},{4,228},{36,4},{8,232},{40,8},{12,236},{44,12},{16,... | collective-permute-start | bytes 110600 | tf_op jit(solution)/shard_map/total/ppermute | solution.py:85
  21.4 4.6 %collective-permute-start.9 = (bf16[48,384]{1,0:T(8,128)(2,1)S(1)}, bf16[48,384]{1,0:T(8,128)(2,1)S(1)}, u32[]{:S(2)}, u32[]{:S(2)}) collective-permute-start(bf16[48,384]{1,0:T(8,128)(2,1)S(1)} %add_convert_fusion.2), channel_id=1, source_target_pairs={{0,32},{32,0},{4,36},{36,4},{8,40},{40,8},{12,44},{44,12},{16,48},... | collective-permute-start | bytes 110600 | tf_op jit(solution)/shard_map/total/ppermute | solution.py:88
  26.0 2.3 %collective-permute-start.14 = (bf16[48,384]{1,0:T(8,128)(2,1)S(1)}, bf16[48,384]{1,0:T(8,128)(2,1)S(1)}, u32[]{:S(2)}, u32[]{:S(2)}) collective-permute-start(bf16[48,384]{1,0:T(8,128)(2,1)S(1)} %add_convert_fusion.1), channel_id=1, source_target_pairs={{32,28},{0,32},{36,24},{4,36},{40,20},{8,40},{44,16},{12,44},{48,1... | collective-permute-start | bytes 110600 | tf_op jit(solution)/shard_map/total/ppermute | solution.py:92
  27.3 1.2 %collective-permute-start.13 = (bf16[48,384]{1,0:T(8,128)(2,1)S(1)}, bf16[48,384]{1,0:T(8,128)(2,1)S(1)}, u32[]{:S(2)}, u32[]{:S(2)}) collective-permute-start(bf16[48,384]{1,0:T(8,128)(2,1)S(1)} %add_convert_fusion.1), channel_id=1, source_target_pairs={{0,32},{32,0},{4,36},{36,4},{8,40},{40,8},{12,44},{44,12},{16,48},... | collective-permute-start | bytes 110600 | tf_op jit(solution)/shard_map/total/ppermute | solution.py:93
  28.5 3.6 %collective-permute-start.15 = (bf16[48,384]{1,0:T(8,128)(2,1)S(1)}, bf16[48,384]{1,0:T(8,128)(2,1)S(1)}, u32[]{:S(2)}, u32[]{:S(2)}) collective-permute-start(bf16[48,384]{1,0:T(8,128)(2,1)S(1)} %add_convert_fusion), channel_id=1, source_target_pairs={{0,32},{32,0},{4,36},{36,4},{8,40},{40,8},{12,44},{44,12},{16,48},... | collective-permute-start | bytes 110600 | tf_op jit(solution)/shard_map/total/ppermute | solution.py:95
